TPU v7x, 256 devices: a whole 4x4x8 slice. The times are simulated.
256 devices in a mesh: dp: 4 (over x), phase: 4 (over y), mp: 16 (over z, core).
Axes of the slice: x: 4, y: 4, z: 8, core: 2. Of those that a mesh axis runs over, the one named last changes fastest.
Arguments:
- prompt_rows: bfloat16 [4, 8, 24, 8192], P('dp', 'phase', None, 'mp'), may hold values from -6 to 6
- row_dest: int32 [4, 8, 24], P(None, 'phase'), may hold values from 0 to 95, as said below
- segment_ids: int32 [4, 4, 48], P('dp'), may hold values from 0 to 5, never falling along the last dimension, each value on 1 to 24 neighbouring positions
- owner: int32 [4, 8, 3, 1], P('dp', 'phase'), may hold values from 0 to 3; in each aligned block of 3 rows (0 to 2, 3 to 5, ..., all dimensions but the last counted through in order) at most 2 rows name the same one
- gain: float32 [4, 8192], P('phase'), may hold values from 0.1 to 1.9
- w_query: bfloat16 [4, 8192, 4096], P('phase', 'dp', 'mp')
- w_key: bfloat16 [4, 8192, 512], P('phase', 'dp', 'mp')
- w_value: bfloat16 [4, 8192, 512], P('phase', 'dp', 'mp'), may hold values from -0.0625 to 0.0625
- w_out: bfloat16 [4, 4096, 8192], P('phase', 'dp', 'mp'), may hold values from -0.09375 to 0.09375
Outputs:
- embeddings: bfloat16 [4, 8, 8, 8192], P('dp', 'phase', None, 'mp')
Inputs may be any that keep to these rules, and one draw needn't show every extreme that they name: `row_dest`: for each half micro-batch t, the values g * 24 + j over all loaders and rows name every group g and slot j exactly once; one loader sends at most 6 rows of one half micro-batch to one group, and every loader sends exactly 6 rows to some group. `segment_ids`: in each micro-batch every prompt number from 0 to 5 appears, on consecutive slots, at most 24 slots each. Within one half micro-batch of one group at most 2 prompts have the same owner, and in some half micro-batch exactly 2 do.
All inputs are finite; a program needn't handle non-finite values.
Results may differ from a plain program's by a relative error of at most 0.015.
Values may be sent and summed in bfloat16 or wider, within the bound.
A program may use at most 64 MiB of HBM per device.

v0:
```python
import jax
import jax.numpy as jnp
from jax import lax
from jax.sharding import PartitionSpec as P

D = 8192
HD = 128
QH = 32
KVH = 4
SEGS = 6
PH = 3


NORM_EPS = 1e-05


def from_behind(value, axis, steps):
    count = lax.axis_size(axis)
    initial, last = (max(0, -steps), min(count, count - steps))
    return lax.ppermute(value, axis, [(source, source + steps) for source in range(initial, last)])


def broadcast(value, axis, root):
    mine = lax.axis_index(axis) == root
    return lax.psum(jnp.where(mine, value, jnp.zeros_like(value)), axis)


def bucket_ranks(labels, buckets):
    hits_table = (labels[..., None] == jnp.arange(buckets, dtype=jnp.int32)).astype(jnp.int32)
    earlier = jnp.cumsum(hits_table, axis=-2) - hits_table
    return jnp.sum(earlier * hits_table, axis=-1)


def attend_heads(query, key_sel, value_sel, segments):
    head_dim = query.shape[2]
    scores = jnp.einsum("qhd,khd->hqk", query, key_sel, preferred_element_type=jnp.float32)
    scores = scores * head_dim ** (-0.5)
    places = jnp.arange(query.shape[0], dtype=jnp.int32)
    allowed = (segments[:, None] == segments[None, :]) & (places[None, :] <= places[:, None])
    scores = jnp.where(allowed[None, :, :], scores, -jnp.inf)
    row_top = jnp.max(scores, axis=2, keepdims=True)
    weights = jnp.exp(scores - row_top)
    probabilities = (weights / jnp.sum(weights, axis=2, keepdims=True)).astype(jnp.bfloat16)
    mixed = jnp.einsum("hqk,khd->qhd", probabilities, value_sel, preferred_element_type=jnp.float32)
    return mixed.astype(jnp.bfloat16).reshape(query.shape[0], -1)


def shards(prompt_rows, row_dest, segment_ids, owner, gain, w_query, w_key, w_value, w_out):
    dp_count = lax.axis_size("dp")
    phase_count = lax.axis_size("phase")
    group_here = lax.axis_index("dp")
    phase_here = lax.axis_index("phase")
    part_here = lax.axis_index("mp")
    halves_here = prompt_rows.shape[1]
    half_rows = prompt_rows.shape[2]
    feature_cols = prompt_rows.shape[3]
    batch_rows = halves_here * half_rows
    capacity = half_rows // min(dp_count, 4)
    half_index = jnp.arange(halves_here, dtype=jnp.int32)[:, None]
    dest_group = row_dest // half_rows
    dest_ranks = bucket_ranks(dest_group, dp_count)
    own_groups = lax.dynamic_index_in_dim(dest_group, group_here, 0, keepdims=False)
    own_ranks = lax.dynamic_index_in_dim(dest_ranks, group_here, 0, keepdims=False)
    send_at = own_groups * capacity + own_ranks
    outgoing = (
        jnp.zeros((halves_here, dp_count * capacity, feature_cols), jnp.bfloat16)
        .at[half_index, send_at]
        .set(prompt_rows[0])
    )
    incoming = lax.all_to_all(
        outgoing.reshape(halves_here, dp_count, capacity, feature_cols),
        "dp",
        split_axis=1,
        concat_axis=1,
        tiled=True,
    )
    source_ids = jnp.arange(dp_count, dtype=jnp.int32)[:, None, None]
    where_from = jnp.transpose(source_ids * capacity + dest_ranks, (1, 0, 2)).reshape(
        halves_here, -1
    )
    target = jnp.where(dest_group == group_here, row_dest % half_rows, half_rows)
    target = jnp.transpose(target, (1, 0, 2)).reshape(halves_here, -1)
    arrived = incoming.reshape(halves_here, dp_count * capacity, feature_cols)[
        half_index, where_from
    ]
    own_halves = (
        jnp.zeros((halves_here, half_rows, feature_cols), jnp.bfloat16)
        .at[half_index, target]
        .set(arrived, mode="drop")
    )
    own_batch = own_halves.reshape(batch_rows, feature_cols)
    waiting = lax.all_gather(own_batch, "phase", axis=0, tiled=True).reshape(
        phase_count, batch_rows, feature_cols
    )
    query_rows, key_rows, value_rows, back_rows = (
        lax.all_gather(w_query[0], "dp", axis=0, tiled=True),
        lax.all_gather(w_key[0], "dp", axis=0, tiled=True),
        lax.all_gather(w_value[0], "dp", axis=0, tiled=True),
        lax.all_gather(w_out[0], "dp", axis=0, tiled=True),
    )
    query_cols = query_rows.shape[1]
    pair_cols = key_rows.shape[1]
    w_proj = jnp.concatenate([query_rows, key_rows, value_rows], axis=1)
    proj_cols = w_proj.shape[1]
    heads_here = query_cols // HD
    group_size = QH // KVH
    key_heads = (part_here * heads_here + jnp.arange(heads_here, dtype=jnp.int32)) // group_size
    gain_row = gain[0]
    segment_table = segment_ids[0]
    last_phase = phase_count - 1
    prompt_numbers = jnp.arange(SEGS, dtype=jnp.int32)

    def advance(tick_index, loop_state):
        current, pooled = loop_state
        batch_index = tick_index - phase_here
        active = (batch_index >= 0) & (batch_index < phase_count)
        batch_slot = jnp.clip(batch_index, 0, phase_count - 1)
        fresh_rows = lax.dynamic_index_in_dim(
            waiting, jnp.clip(tick_index, 0, phase_count - 1), 0, keepdims=False
        )
        tok_rows = jnp.where(phase_here == 0, fresh_rows, current)
        tok_segments = lax.dynamic_index_in_dim(segment_table, batch_slot, 0, keepdims=False)
        tok_float = tok_rows.astype(jnp.float32)
        whole_rows = lax.all_gather(tok_rows, "mp", axis=1, tiled=True)
        whole_float = whole_rows.astype(jnp.float32)
        squares = jnp.sum(whole_float * whole_float, axis=1)
        projected = lax.cond(
            active,
            lambda: jnp.dot(
                (whole_float * gain_row[None, :]).astype(jnp.bfloat16),
                w_proj,
                preferred_element_type=jnp.float32,
            ),
            lambda: jnp.zeros((batch_rows, proj_cols), jnp.float32),
        )
        qkv_rows = (projected * lax.rsqrt(squares / D + NORM_EPS)[:, None]).astype(jnp.bfloat16)
        query = qkv_rows[:, :query_cols].reshape(batch_rows, heads_here, HD)
        key_own = qkv_rows[:, query_cols : query_cols + pair_cols]
        value_own = qkv_rows[:, query_cols + pair_cols :]
        key_all, value_all = (
            lax.all_gather(key_own, "mp", axis=1, tiled=True),
            lax.all_gather(value_own, "mp", axis=1, tiled=True),
        )
        key_sel = jnp.take(key_all.reshape(batch_rows, KVH, HD), key_heads, axis=1)
        value_sel = jnp.take(value_all.reshape(batch_rows, KVH, HD), key_heads, axis=1)
        mixed_own = attend_heads(query, key_sel, value_sel, tok_segments)
        mixed = lax.all_gather(mixed_own, "mp", axis=1, tiled=True)
        updated = lax.cond(
            active,
            lambda: (
                tok_float + jnp.dot(mixed, back_rows, preferred_element_type=jnp.float32)
            ).astype(jnp.bfloat16),
            lambda: tok_rows,
        )
        segment_hits = tok_segments[None, :] == prompt_numbers[:, None]
        segment_sums = jnp.dot(
            segment_hits.astype(jnp.bfloat16), updated, preferred_element_type=jnp.float32
        )
        counts = jnp.sum(segment_hits.astype(jnp.float32), axis=1)
        segment_means = segment_sums / counts[:, None]
        store_here = active & (phase_here == last_phase)
        stored = lax.dynamic_index_in_dim(pooled, batch_slot, 0, keepdims=False)
        pooled = lax.dynamic_update_index_in_dim(
            pooled, jnp.where(store_here, segment_means, stored), batch_slot, 0
        )
        passed = from_behind(updated, "phase", 1)
        return (passed, pooled)

    start_state = (
        jnp.zeros((batch_rows, feature_cols), jnp.bfloat16),
        jnp.zeros((phase_count, SEGS, feature_cols), jnp.float32),
    )
    current, pooled = lax.fori_loop(0, phase_count + phase_count - 1, advance, start_state)
    shared = broadcast(pooled.astype(jnp.bfloat16), "phase", last_phase)
    own_prompts = lax.dynamic_index_in_dim(shared, phase_here, 0, keepdims=False).reshape(
        halves_here, PH, feature_cols
    )
    owner_ids = owner[0, :, :, 0]
    return_cap = max(2, PH // min(dp_count, 4))
    send_slots = owner_ids * return_cap + bucket_ranks(owner_ids, dp_count)
    parcel = (
        jnp.zeros((halves_here, dp_count * return_cap, feature_cols), jnp.bfloat16)
        .at[half_index, send_slots]
        .set(own_prompts)
    )
    returned = lax.all_to_all(
        parcel.reshape(halves_here, dp_count, return_cap, feature_cols),
        "dp",
        split_axis=1,
        concat_axis=1,
        tiled=True,
    )
    return returned.reshape(1, halves_here, dp_count * return_cap, feature_cols)


def solution(mesh):
    in_specs = (
        P("dp", "phase", None, "mp"),
        P(None, "phase", None),
        P("dp", None, None),
        P("dp", "phase", None, None),
        P("phase", None),
        P("phase", "dp", "mp"),
        P("phase", "dp", "mp"),
        P("phase", "dp", "mp"),
        P("phase", "dp", "mp"),
    )
    out_specs = P("dp", "phase", None, "mp")
    return jax.shard_map(shards, mesh=mesh, in_specs=in_specs, out_specs=out_specs, check_vma=False)
```

profile of v0, /device:TPU:25, one launch (start us, length us, event | category | flops | bytes accessed | tf_op | source)
XLA Modules:
  0.0 739.7 jit_solution(5874868909846574600)
XLA Ops:
  9.3 4.6 scatter_fusion
  14.6 4.0 all-to-all-start
  20.8 34.0 %all-gather.1 = bf16[1,8192,32]{2,1,0:T(8,128)(2,1)S(1)} all-gather(bf16[1,2048,32]{2,1,0:T(8,128)(2,1)S(1)} %copy.99), channel_id=3, replica_groups=mesh['dp'=4,'phase'=4,'mp'=16] {'dp'}, dimensions={1}, use_global_device_ids=true | all-gather | bytes 655360 | tf_op jit(solution)/shard_map/all_gather | solution.py:97
  54.8 36.7 %all-gather.2 = bf16[1,8192,32]{2,1,0:T(8,128)(2,1)} all-gather(bf16[1,2048,32]{2,1,0:T(8,128)(2,1)S(1)} %copy.100), channel_id=4, replica_groups=mesh['dp'=4,'phase'=4,'mp'=16] {'dp'}, dimensions={1}, use_global_device_ids=true | all-gather | bytes 655360 | tf_op jit(solution)/shard_map/all_gather | solution.py:98
  91.8 2.7 gather_fusion.2
  94.5 11.3 %scatter_fusion.1 = bf16[2,24,512]{2,1,0:T(8,128)(2,1)S(1)} fusion(bf16[2,24,512]{2,1,0:T(8,128)(2,1)S(1)} %broadcast.214, s32[192]{0:T(256)S(1)} %reshape.289, bf16[192,512]{1,0:T(8,128)(2,1)S(1)} %gather_fusion.2), kind=kCustom, calls=%fused_computation.4 | custom fusion | bytes 591360 | tf_op jit(solution)/shard_map/scatter | solution.py:89
  105.8 10.3 %all_gather.47 = bf16[192,512]{1,0:T(8,128)(2,1)S(1)} all-gather(bf16[48,512]{1,0:T(8,128)(2,1)S(1)} %bitcast.97), channel_id=1, replica_groups=mesh['dp'=4,'phase'=4,'mp'=16] {'phase'}, dimensions={0}, use_global_device_ids=true | all-gather | bytes 245760 | tf_op jit(solution)/shard_map/all_gather | solution.py:92
  116.1 8.0 %pad_maximum_fusion = bf16[8192,320]{1,0:T(8,128)(2,1)} fusion(bf16[8192,32]{1,0:T(8,128)(2,1)} %bitcast.101, bf16[8192,32]{1,0:T(8,128)(2,1)S(1)} %bitcast.100, bf16[8192,256]{1,0:T(8,128)(2,1)} %bitcast.103), kind=kLoop, calls=%fused_computation.57 | loop fusion | flops 15728640 | bytes 10485760 | tf_op jit(solution)/shard_map/concatenate | solution.py:103
  124.1 20.0 %all-gather.9.cloned.1.call-done = bf16[1,4096,512]{2,1,0:T(8,128)(2,1)} async-done(((bf16[1,1024,512]{2,1,0:T(8,128)(2,1)}), bf16[1,4096,512]{2,1,0:T(8,128)(2,1)}) %all-gather.9.cloned.1.call-update) | async-done | bytes 4194320 | tf_op jit(solution)/shard_map/all_gather | solution.py:99
  144.1 569.5 %while.17 = (s32[]{:T(128)}, bf16[48,512]{1,0:T(8,128)(2,1)S(1)}, bf16[4,6,512]{2,1,0:T(8,128)(2,1)S(1)}, s32[]{:T(128)}, pred[]{:T(512)}, /*index=5*/bf16[4,48,...) while((s32[]{:T(128)}, bf16[48,512]{1,0:T(8,128)(2,1)S(1)}, ...), condition=%wide.region_15.17_spmd.clone, body=%wide.region_6.16_spmd.clone.sunk | while | flops 458212032 | bytes 17332396 | solution.py:173
  144.2 20.1 %all_gather.60 = bf16[48,8192]{1,0:T(8,128)(2,1)S(1)} all-gather(bf16[48,512]{1,0:T(8,128)(2,1)S(1)} %get-tuple-element.417), channel_id=1, replica_groups=mesh['dp'=4,'phase'=4,'mp'=16] {'mp'}, dimensions={1}, use_global_device_ids=true | all-gather | bytes 835584 | tf_op jit(solution)/shard_map/while/body/eval_jaxpr/all_gather | solution.py:124
  164.8 15.3 %all_gather.62 = bf16[48,512]{0,1:T(8,128)(2,1)S(1)} all-gather(bf16[48,32]{0,1:T(8,128)(2,1)S(1)} %get-tuple-element.420), channel_id=1, replica_groups=mesh['dp'=4,'phase'=4,'mp'=16] {'mp'}, dimensions={1}, use_global_device_ids=true | all-gather | bytes 52224 | tf_op jit(solution)/shard_map/while/body/eval_jaxpr/all_gather | solution.py:141
  181.8 15.6 %all_gather.61 = bf16[48,512]{0,1:T(8,128)(2,1)S(1)} all-gather(bf16[48,32]{0,1:T(8,128)(2,1)S(1)} %get-tuple-element.419), channel_id=1, replica_groups=mesh['dp'=4,'phase'=4,'mp'=16] {'mp'}, dimensions={1}, use_global_device_ids=true | all-gather | bytes 52224 | tf_op jit(solution)/shard_map/while/body/eval_jaxpr/all_gather | solution.py:142
  198.4 16.1 %all_gather.63 = bf16[48,4096]{1,0:T(8,128)(2,1)S(1)} all-gather(bf16[48,256]{1,0:T(8,128)(2,1)S(1)} %bitcast.104), channel_id=1, replica_groups=mesh['dp'=4,'phase'=4,'mp'=16] {'mp'}, dimensions={1}, use_global_device_ids=true | all-gather | bytes 417792 | tf_op jit(solution)/shard_map/while/body/eval_jaxpr/all_gather | solution.py:147
  216.0 3.3 collective-permute-done
  219.3 18.6 %all_gather.60 = bf16[48,8192]{1,0:T(8,128)(2,1)S(1)} all-gather(bf16[48,512]{1,0:T(8,128)(2,1)S(1)} %get-tuple-element.417), channel_id=1, replica_groups=mesh['dp'=4,'phase'=4,'mp'=16] {'mp'}, dimensions={1}, use_global_device_ids=true | all-gather | bytes 835584 | tf_op jit(solution)/shard_map/while/body/eval_jaxpr/all_gather | solution.py:124
  238.4 15.3 %all_gather.62 = bf16[48,512]{0,1:T(8,128)(2,1)S(1)} all-gather(bf16[48,32]{0,1:T(8,128)(2,1)S(1)} %get-tuple-element.420), channel_id=1, replica_groups=mesh['dp'=4,'phase'=4,'mp'=16] {'mp'}, dimensions={1}, use_global_device_ids=true | all-gather | bytes 52224 | tf_op jit(solution)/shard_map/while/body/eval_jaxpr/all_gather | solution.py:141
  255.4 15.6 %all_gather.61 = bf16[48,512]{0,1:T(8,128)(2,1)S(1)} all-gather(bf16[48,32]{0,1:T(8,128)(2,1)S(1)} %get-tuple-element.419), channel_id=1, replica_groups=mesh['dp'=4,'phase'=4,'mp'=16] {'mp'}, dimensions={1}, use_global_device_ids=true | all-gather | bytes 52224 | tf_op jit(solution)/shard_map/while/body/eval_jaxpr/all_gather | solution.py:142
  271.9 16.1 %all_gather.63 = bf16[48,4096]{1,0:T(8,128)(2,1)S(1)} all-gather(bf16[48,256]{1,0:T(8,128)(2,1)S(1)} %bitcast.104), channel_id=1, replica_groups=mesh['dp'=4,'phase'=4,'mp'=16] {'mp'}, dimensions={1}, use_global_device_ids=true | all-gather | bytes 417792 | tf_op jit(solution)/shard_map/while/body/eval_jaxpr/all_gather | solution.py:147
  289.5 3.3 collective-permute-done
  292.8 18.6 %all_gather.60 = bf16[48,8192]{1,0:T(8,128)(2,1)S(1)} all-gather(bf16[48,512]{1,0:T(8,128)(2,1)S(1)} %get-tuple-element.417), channel_id=1, replica_groups=mesh['dp'=4,'phase'=4,'mp'=16] {'mp'}, dimensions={1}, use_global_device_ids=true | all-gather | bytes 835584 | tf_op jit(solution)/shard_map/while/body/eval_jaxpr/all_gather | solution.py:124
  311.9 15.3 %all_gather.62 = bf16[48,512]{0,1:T(8,128)(2,1)S(1)} all-gather(bf16[48,32]{0,1:T(8,128)(2,1)S(1)} %get-tuple-element.420), channel_id=1, replica_groups=mesh['dp'=4,'phase'=4,'mp'=16] {'mp'}, dimensions={1}, use_global_device_ids=true | all-gather | bytes 52224 | tf_op jit(solution)/shard_map/while/body/eval_jaxpr/all_gather | solution.py:141
  329.0 15.6 %all_gather.61 = bf16[48,512]{0,1:T(8,128)(2,1)S(1)} all-gather(bf16[48,32]{0,1:T(8,128)(2,1)S(1)} %get-tuple-element.419), channel_id=1, replica_groups=mesh['dp'=4,'phase'=4,'mp'=16] {'mp'}, dimensions={1}, use_global_device_ids=true | all-gather | bytes 52224 | tf_op jit(solution)/shard_map/while/body/eval_jaxpr/all_gather | solution.py:142
  345.5 16.1 %all_gather.63 = bf16[48,4096]{1,0:T(8,128)(2,1)S(1)} all-gather(bf16[48,256]{1,0:T(8,128)(2,1)S(1)} %bitcast.104), channel_id=1, replica_groups=mesh['dp'=4,'phase'=4,'mp'=16] {'mp'}, dimensions={1}, use_global_device_ids=true | all-gather | bytes 417792 | tf_op jit(solution)/shard_map/while/body/eval_jaxpr/all_gather | solution.py:147
  363.1 24.2 %collective-permute-done = bf16[48,512]{1,0:T(8,128)(2,1)S(1)} collective-permute-done((bf16[48,512]{1,0:T(8,128)(2,1)S(1)}, bf16[48,512]{1,0:T(8,128)(2,1)S(1)}, u32[]{:S(2)}, u32[]{:S(2)}) %collective-permute-start) | collective-permute-done | bytes 49184 | tf_op jit(solution)/shard_map/while/body/eval_jaxpr/ppermute | solution.py:20
  387.3 18.0 %all_gather.60 = bf16[48,8192]{1,0:T(8,128)(2,1)S(1)} all-gather(bf16[48,512]{1,0:T(8,128)(2,1)S(1)} %get-tuple-element.417), channel_id=1, replica_groups=mesh['dp'=4,'phase'=4,'mp'=16] {'mp'}, dimensions={1}, use_global_device_ids=true | all-gather | bytes 835584 | tf_op jit(solution)/shard_map/while/body/eval_jaxpr/all_gather | solution.py:124
  405.7 5.2 conditional.6
  405.7 5.2 fusion.4
  410.9 15.3 %all_gather.62 = bf16[48,512]{0,1:T(8,128)(2,1)S(1)} all-gather(bf16[48,32]{0,1:T(8,128)(2,1)S(1)} %get-tuple-element.420), channel_id=1, replica_groups=mesh['dp'=4,'phase'=4,'mp'=16] {'mp'}, dimensions={1}, use_global_device_ids=true | all-gather | bytes 52224 | tf_op jit(solution)/shard_map/while/body/eval_jaxpr/all_gather | solution.py:141
  428.0 15.6 %all_gather.61 = bf16[48,512]{0,1:T(8,128)(2,1)S(1)} all-gather(bf16[48,32]{0,1:T(8,128)(2,1)S(1)} %get-tuple-element.419), channel_id=1, replica_groups=mesh['dp'=4,'phase'=4,'mp'=16] {'mp'}, dimensions={1}, use_global_device_ids=true | all-gather | bytes 52224 | tf_op jit(solution)/shard_map/while/body/eval_jaxpr/all_gather | solution.py:142
  444.5 16.1 %all_gather.63 = bf16[48,4096]{1,0:T(8,128)(2,1)S(1)} all-gather(bf16[48,256]{1,0:T(8,128)(2,1)S(1)} %bitcast.104), channel_id=1, replica_groups=mesh['dp'=4,'phase'=4,'mp'=16] {'mp'}, dimensions={1}, use_global_device_ids=true | all-gather | bytes 417792 | tf_op jit(solution)/shard_map/while/body/eval_jaxpr/all_gather | solution.py:147
  460.6 3.0 conditional.7
  460.6 3.0 fusion.6
  465.1 3.4 collective-permute-done
  468.5 18.5 %all_gather.60 = bf16[48,8192]{1,0:T(8,128)(2,1)S(1)} all-gather(bf16[48,512]{1,0:T(8,128)(2,1)S(1)} %get-tuple-element.417), channel_id=1, replica_groups=mesh['dp'=4,'phase'=4,'mp'=16] {'mp'}, dimensions={1}, use_global_device_ids=true | all-gather | bytes 835584 | tf_op jit(solution)/shard_map/while/body/eval_jaxpr/all_gather | solution.py:124
  487.4 5.2 conditional.6
  487.4 5.2 fusion.4
  492.7 15.3 %all_gather.62 = bf16[48,512]{0,1:T(8,128)(2,1)S(1)} all-gather(bf16[48,32]{0,1:T(8,128)(2,1)S(1)} %get-tuple-element.420), channel_id=1, replica_groups=mesh['dp'=4,'phase'=4,'mp'=16] {'mp'}, dimensions={1}, use_global_device_ids=true | all-gather | bytes 52224 | tf_op jit(solution)/shard_map/while/body/eval_jaxpr/all_gather | solution.py:141
  509.7 15.6 %all_gather.61 = bf16[48,512]{0,1:T(8,128)(2,1)S(1)} all-gather(bf16[48,32]{0,1:T(8,128)(2,1)S(1)} %get-tuple-element.419), channel_id=1, replica_groups=mesh['dp'=4,'phase'=4,'mp'=16] {'mp'}, dimensions={1}, use_global_device_ids=true | all-gather | bytes 52224 | tf_op jit(solution)/shard_map/while/body/eval_jaxpr/all_gather | solution.py:142
  526.2 16.1 %all_gather.63 = bf16[48,4096]{1,0:T(8,128)(2,1)S(1)} all-gather(bf16[48,256]{1,0:T(8,128)(2,1)S(1)} %bitcast.104), channel_id=1, replica_groups=mesh['dp'=4,'phase'=4,'mp'=16] {'mp'}, dimensions={1}, use_global_device_ids=true | all-gather | bytes 417792 | tf_op jit(solution)/shard_map/while/body/eval_jaxpr/all_gather | solution.py:147
  542.3 3.0 conditional.7
  542.3 3.0 fusion.6
  545.3 1.3 collective-permute-start
  546.9 3.4 collective-permute-done
  550.3 18.5 %all_gather.60 = bf16[48,8192]{1,0:T(8,128)(2,1)S(1)} all-gather(bf16[48,512]{1,0:T(8,128)(2,1)S(1)} %get-tuple-element.417), channel_id=1, replica_groups=mesh['dp'=4,'phase'=4,'mp'=16] {'mp'}, dimensions={1}, use_global_device_ids=true | all-gather | bytes 835584 | tf_op jit(solution)/shard_map/while/body/eval_jaxpr/all_gather | solution.py:124
  569.1 5.2 conditional.6
  569.1 5.2 fusion.4
  574.4 15.3 %all_gather.62 = bf16[48,512]{0,1:T(8,128)(2,1)S(1)} all-gather(bf16[48,32]{0,1:T(8,128)(2,1)S(1)} %get-tuple-element.420), channel_id=1, replica_groups=mesh['dp'=4,'phase'=4,'mp'=16] {'mp'}, dimensions={1}, use_global_device_ids=true | all-gather | bytes 52224 | tf_op jit(solution)/shard_map/while/body/eval_jaxpr/all_gather | solution.py:141
  591.4 15.6 %all_gather.61 = bf16[48,512]{0,1:T(8,128)(2,1)S(1)} all-gather(bf16[48,32]{0,1:T(8,128)(2,1)S(1)} %get-tuple-element.419), channel_id=1, replica_groups=mesh['dp'=4,'phase'=4,'mp'=16] {'mp'}, dimensions={1}, use_global_device_ids=true | all-gather | bytes 52224 | tf_op jit(solution)/shard_map/while/body/eval_jaxpr/all_gather | solution.py:142
  607.9 16.1 %all_gather.63 = bf16[48,4096]{1,0:T(8,128)(2,1)S(1)} all-gather(bf16[48,256]{1,0:T(8,128)(2,1)S(1)} %bitcast.104), channel_id=1, replica_groups=mesh['dp'=4,'phase'=4,'mp'=16] {'mp'}, dimensions={1}, use_global_device_ids=true | all-gather | bytes 417792 | tf_op jit(solution)/shard_map/while/body/eval_jaxpr/all_gather | solution.py:147
  624.0 3.0 conditional.7
  624.0 3.0 fusion.6
  628.6 3.4 collective-permute-done
  632.0 18.5 %all_gather.60 = bf16[48,8192]{1,0:T(8,128)(2,1)S(1)} all-gather(bf16[48,512]{1,0:T(8,128)(2,1)S(1)} %get-tuple-element.417), channel_id=1, replica_groups=mesh['dp'=4,'phase'=4,'mp'=16] {'mp'}, dimensions={1}, use_global_device_ids=true | all-gather | bytes 835584 | tf_op jit(solution)/shard_map/while/body/eval_jaxpr/all_gather | solution.py:124
  650.9 5.2 conditional.6
  650.9 5.2 fusion.4
  656.1 15.3 %all_gather.62 = bf16[48,512]{0,1:T(8,128)(2,1)S(1)} all-gather(bf16[48,32]{0,1:T(8,128)(2,1)S(1)} %get-tuple-element.420), channel_id=1, replica_groups=mesh['dp'=4,'phase'=4,'mp'=16] {'mp'}, dimensions={1}, use_global_device_ids=true | all-gather | bytes 52224 | tf_op jit(solution)/shard_map/while/body/eval_jaxpr/all_gather | solution.py:141
  673.2 15.6 %all_gather.61 = bf16[48,512]{0,1:T(8,128)(2,1)S(1)} all-gather(bf16[48,32]{0,1:T(8,128)(2,1)S(1)} %get-tuple-element.419), channel_id=1, replica_groups=mesh['dp'=4,'phase'=4,'mp'=16] {'mp'}, dimensions={1}, use_global_device_ids=true | all-gather | bytes 52224 | tf_op jit(solution)/shard_map/while/body/eval_jaxpr/all_gather | solution.py:142
  689.7 16.1 %all_gather.63 = bf16[48,4096]{1,0:T(8,128)(2,1)S(1)} all-gather(bf16[48,256]{1,0:T(8,128)(2,1)S(1)} %bitcast.104), channel_id=1, replica_groups=mesh['dp'=4,'phase'=4,'mp'=16] {'mp'}, dimensions={1}, use_global_device_ids=true | all-gather | bytes 417792 | tf_op jit(solution)/shard_map/while/body/eval_jaxpr/all_gather | solution.py:147
  705.8 3.0 conditional.7
  705.8 3.0 fusion.6
  710.3 3.3 collective-permute-done
  713.6 10.6 %psum.7 = bf16[4,6,512]{2,1,0:T(8,128)(2,1)S(1)} all-reduce(bf16[4,6,512]{2,1,0:T(8,128)(2,1)S(1)} %convert_select_fusion), channel_id=1, replica_groups=mesh['dp'=4,'phase'=4,'mp'=16] {'phase'}, use_global_device_ids=true, to_apply=%region_16.18 | all-reduce | flops 12288 | bytes 49152 | tf_op jit(solution)/shard_map/psum | solution.py:25
  725.1 7.1 all_to_all.10
  (225 shorter events, 37.8 us)
Async XLA Ops:
  6.5 13.5 %copy-start.1 = (bf16[1,2048,32]{1,2,0:T(8,128)(2,1)S(1)}, bf16[1,2048,32]{1,2,0:T(8,128)(2,1)}, u32[]{:S(2)}) copy-start(bf16[1,2048,32]{1,2,0:T(8,128)(2,1)} %param.24) | copy-start | bytes 393220
  6.5 13.8 %copy-start.2 = (s32[1,2,3,1]{2,3,1,0:T(1,128)S(1)}, s32[1,2,3,1]{2,3,1,0:T(1,128)}, u32[]{:S(2)}) copy-start(s32[1,2,3,1]{2,3,1,0:T(1,128)} %param.20) | copy-start | bytes 76
  6.5 109.6 %all-gather.7.cloned.1.call-start = ((), (), s32[]{:S(2)}) async-start(), calls=%async_computation.2 | async-start | bytes 5242880 | tf_op jit(solution)/shard_map/all_gather | solution.py:96
  7.3 136.9 %all-gather.9.cloned.1.call-start = ((), (), s32[]{:S(2)}) async-start(), calls=%async_computation.3 | async-start | bytes 5242880 | tf_op jit(solution)/shard_map/all_gather | solution.py:99
  14.6 77.2 %all-to-all-start = ((bf16[2,4,6,512]{3,0,2,1:T(2,128)(2,1)}), bf16[2,4,6,512]{3,0,2,1:T(2,128)(2,1)S(1)}, u32[]{:S(2)}, u32[]{:S(2)}) async-start(bf16[2,4,6,512]{3,0,2,1:T(2,128)(2,1)} %bitcast.7), calls=%async_computation | async-start | bytes 98304 | tf_op jit(solution)/shard_map/all_to_all | solution.py:70
  116.1 28.0 %copy-start = (f32[1,8192]{1,0:T(1,128)S(1)}, f32[1,8192]{1,0:T(1,128)}, u32[]{:S(2)}) copy-start(f32[1,8192]{1,0:T(1,128)} %param.21) | copy-start | bytes 98308
  214.4 4.8 collective-permute-start
  288.0 4.8 collective-permute-start
  361.5 25.7 %collective-permute-start = (bf16[48,512]{1,0:T(8,128)(2,1)S(1)}, bf16[48,512]{1,0:T(8,128)(2,1)S(1)}, u32[]{:S(2)}, u32[]{:S(2)}) collective-permute-start(bf16[48,512]{1,0:T(8,128)(2,1)S(1)} %get-tuple-element.472), channel_id=1, source_target_pairs={{0,16},{16,32},{32,48},{1,17},{17,33},{33,49},{2,18},{18,34},{34,5... | collective-permute-start | bytes 147464 | tf_op jit(solution)/shard_map/while/body/eval_jaxpr/ppermute | solution.py:20
  463.6 4.9 collective-permute-start
  545.3 4.9 collective-permute-start
  627.0 4.9 collective-permute-start
  708.8 4.8 collective-permute-start
Sparse Core Ops, SparseCore 0:
  9.2 82.9 all-gather.6
  93.9 50.1 all-gather.8
where the time goes:
time: 749 us; the launch traced here: 740 us
  blocking collectives  559 us (75%)
  waiting for transfers between devices  65.5 us (9%)
  local copies, waits for them, and re-layouts  37.2 us (5%)
  matrix products  36.4 us (5%)
  other arithmetic  14.2 us (2%)
  between operations  13.6 us (2%)
  starting transfers between devices  13.1 us (2%)
    all_gather x7, blocking collectives, advance(): whole_rows = lax.all_gather(tok_rows, 'mp', axis=1, tiled=True)  131 us
    all_gather x7, blocking collectives, advance(): mixed = lax.all_gather(mixed_own, 'mp', axis=1, tiled=True)  113 us
    all_gather x7, blocking collectives, advance(): lax.all_gather(value_own, 'mp', axis=1, tiled=True)  109 us
    all_gather x7, blocking collectives, advance(): lax.all_gather(key_own, 'mp', axis=1, tiled=True)  107 us
    ppermute x7, waiting for transfers between devices, from_behind(): lax.ppermute(value, axis, [(source, source + steps) for source in range(i...  44.1 us
    all_gather x1, blocking collectives, shards(): lax.all_gather(w_value[0], 'dp', axis=0, tiled=True)  36.7 us
    all_gather x1, blocking collectives, shards(): lax.all_gather(w_key[0], 'dp', axis=0, tiled=True)  34 us
    cond x4, matrix products, advance(): lax.cond(active, lambda: jnp.dot((whole_float * gain_row[None, :]).astype...  20.6 us
  transfers between devices with their start and end apart: 10, of which 8 were waited for; matrix products, arithmetic and copies ran while one was open for 4% of the time, Pallas kernels for 0%

commit v1 on v0

v1 whole, which is shorter than its diff:
```python
import jax
import jax.numpy as jnp
from jax import lax
from jax.experimental import pallas as pl
from jax.experimental.pallas import tpu as pltpu
from jax.sharding import PartitionSpec as P

MESH = pl.DeviceIdType.MESH
F32 = jnp.float32
BF16 = jnp.bfloat16
I32 = jnp.int32

D = 8192
HD = 128
MB = 48
M = 4
NX = 4
NZ = 8
EPS = 1e-05
BLK = 512


def iota(shape, dim):
    return lax.broadcasted_iota(I32, shape, dim)


def dot(a, b):
    return jnp.dot(a, b, preferred_element_type=F32)


def dot_nt(a, b):
    return lax.dot_general(a, b, (((1,), (1,)), ((), ())), preferred_element_type=F32)


def to_row(col):
    eye = iota((MB, 128), 0) == iota((MB, 128), 1)
    return jnp.sum(jnp.where(eye, col, 0.0), axis=0, keepdims=True)


def to_col(row):
    eye = iota((MB, MB), 0) == iota((MB, MB), 1)
    return jnp.sum(jnp.where(eye, row, 0.0), axis=1, keepdims=True)


def kernel(
    rows, row_dest, segs, owner, gain, wq, wk, wv, wo, out,
    raw, seg, code, wq_v, wk_v, wv_v, kvt, wkv_v, wo_v,
    hid, q_out, q_in, s_out, s_in, mx, mixed, o_out, o_in, h_out, e_out, e_in,
    loc, one_s, one_r, x3_s, x3_r, kv_s, kv_r, pro_s, h_r,
    q_s, q_r, s_s, s_r, mx_s, mx_r, o_s, o_r, h_s, e_s, e_r,
):
    x = lax.axis_index("dp")
    y = lax.axis_index("phase")
    p = lax.axis_index("mp")
    z = p // 2
    c = p % 2
    ring = z // 2
    odd = z % 2

    def at(xx, yy, zz, cc):
        return (xx, yy, zz * 2 + cc)

    def remote(src, dst, send, recv, device):
        return pltpu.make_async_remote_copy(
            src_ref=src, dst_ref=dst, send_sem=send, recv_sem=recv,
            device_id=device, device_id_type=MESH,
        )

    def local(src, dst, sem):
        return pltpu.make_async_copy(src, dst, sem)

    def settle(ref, sem):
        pltpu.make_async_copy(ref, ref, sem).wait()

    def turn(k):
        return (x + k) % NX

    loads = [
        local(rows, raw.at[x], loc.at[0]),
        local(wk, wk_v, loc.at[1]),
        local(wv, wv_v, loc.at[2]),
        local(wq, wq_v.at[c], loc.at[3]),
        local(wo, wo_v.at[c], loc.at[4]),
    ]
    for load in loads:
        load.start()

    barrier = pltpu.get_barrier_semaphore()

    def greet(device):
        pl.semaphore_signal(barrier, inc=1, device_id=device, device_id_type=MESH)

    pair_z = z + 1 - 2 * odd
    self_mx = x == ring
    self_pro = (y == 0) & (x == ring) & (c == x // 2)
    self_e = (y == 3) & (x % 2 == c)
    greet(at(x, y, z, 1 - c))
    greet(at(x, y, pair_z, 0))
    greet(at(x, y, pair_z, 1))
    for k in range(1, NX):
        greet(at(turn(k), y, z, c))
    for r in range(NX):
        for e in range(2):
            @pl.when(jnp.logical_not((x == r) & (2 * x + e == z)))
            def _():
                greet(at(r, y, 2 * x + e, c))

    @pl.when(y > 0)
    def _():
        for r in range(NX):
            for e in range(2):
                greet(at(r, y - 1, 2 * x + e, c))

    @pl.when(y == 0)
    def _():
        for f in range(M):
            for gg in range(2):
                for e in range(2):
                    for cc in range(2):
                        if f == 0:
                            @pl.when(jnp.logical_not((2 * c + gg == x) & (2 * x + e == z) & (c == cc)))
                            def _():
                                greet(at(2 * c + gg, f, 2 * x + e, cc))
                        else:
                            greet(at(2 * c + gg, f, 2 * x + e, cc))

    for b in range(2):
        for cc in range(2):
            @pl.when(jnp.logical_not((y == 3) & (c + 2 * b == x) & (c == cc)))
            def _():
                greet(at(c + 2 * b, 3, z, cc))

    seg[x] = jnp.zeros((8, 128), I32)
    seg[x, 0:4, 0:MB] = segs[0]
    lane = iota((8, 128), 1)
    table = jnp.full((8, 128), -1, I32)
    for t in range(2):
        for i in range(3):
            who = owner[t, i]
            rank = jnp.int32(0)
            for before in range(i):
                rank = rank + (owner[t, before] == who).astype(I32)
            table = jnp.where(lane == 3 * t + i, 2 * who + rank, table)
    code[x] = table

    count = 22 - self_mx.astype(I32) - self_pro.astype(I32)
    count = count + jnp.where(y < 3, 8, 16) - self_e.astype(I32)
    pl.semaphore_wait(barrier, count)

    loads[0].wait()
    for k in range(1, NX):
        remote(raw.at[x], raw.at[x], x3_s.at[0], x3_r.at[0], at(turn(k), y, z, c)).start()
    for k in range(1, NX):
        remote(seg.at[x], seg.at[x], x3_s.at[1], x3_r.at[1], at(turn(k), y, z, c)).start()
        remote(code.at[x], code.at[x], x3_s.at[2], x3_r.at[2], at(turn(k), y, z, c)).start()
    loads[3].wait()
    remote(wq_v.at[c], wq_v.at[c], one_s.at[0], one_r.at[0], at(x, y, z, 1 - c)).start()
    loads[4].wait()
    remote(wo_v.at[c], wo_v.at[c], one_s.at[1], one_r.at[1], at(x, y, z, 1 - c)).start()

    loads[1].wait()
    loads[2].wait()
    quad = 2 * odd + c
    kvt[quad, 0] = wk_v[...].T
    kvt[quad, 1] = wv_v[...].T
    mine = kvt.at[quad]
    remote(mine, mine, kv_s, kv_r, at(x, y, z, 1 - c)).start()
    remote(mine, mine, kv_s, kv_r, at(x, y, pair_z, 0)).start()
    remote(mine, mine, kv_s, kv_r, at(x, y, pair_z, 1)).start()

    settle(raw.at[0:3], x3_r.at[0])
    dest = row_dest[...].astype(F32)
    spread = [
        (iota((24, MB), 0) + 24 * t == iota((24, MB), 1)).astype(F32) for t in range(2)
    ]
    dest = dot(dest[:, 0, :], spread[0]) + dot(dest[:, 1, :], spread[1])
    slot = iota((MB, MB), 0)
    place = iota((MB, MB), 1)
    upper = slot >= 24
    wanted = (slot - jnp.where(upper, 24, 0) + 24 * x).astype(F32)
    same_half = upper == (place >= 24)
    packed = jnp.zeros((MB, BLK), F32)
    for l in range(NX):
        hits = same_half & (dest[l : l + 1, :] == wanted)
        packed = packed + dot(hits.astype(BF16), raw[l])
    h_out[y] = packed.astype(BF16)
    first = hid.at[y, (x % 2) * 4 + quad]

    @pl.when(self_pro)
    def _():
        local(h_out.at[y], first, h_r.at[y]).start()

    @pl.when(jnp.logical_not(self_pro))
    def _():
        remote(h_out.at[y], first, pro_s.at[0], h_r.at[y], at(ring, 0, z, x // 2)).start()

    for dz in range(1, NZ):
        remote(
            h_out.at[y], first, pro_s.at[1], h_r.at[y], at(ring, 0, (z + dz) % NZ, x // 2)
        ).start()

    settle(kvt.at[0:3], kv_r)
    for t in range(2):
        wkv_v[:, 128 * t : 128 * t + 128] = jnp.concatenate(
            [kvt[j, t] for j in range(4)], axis=0
        ).T
    settle(wq_v.at[0], one_r.at[0])
    settle(wo_v.at[0], one_r.at[1])
    settle(seg.at[0:3], x3_r.at[1])
    settle(code.at[0:3], x3_r.at[2])

    group = 2 * c + x // 2
    block = (x // 2) * 4 + 2 * odd + x % 2

    def project(m):
        settle(hid.at[m], h_r.at[m])
        squares = jnp.zeros((2 * MB, 128), F32)
        sums = [jnp.zeros((2 * MB, 256), F32) for _ in range(3)]
        for j in range(4):
            h = jnp.concatenate([hid[m, j], hid[m, 4 + j]], axis=0).astype(F32)
            square = h * h
            for i in range(4):
                squares = squares + square[:, 128 * i : 128 * i + 128]
            g = gain[:, pl.ds(pl.multiple_of(x * 2048 + BLK * j, BLK), BLK)]
            gated = (h * g).astype(BF16)
            ks = slice(BLK * j, BLK * j + BLK)
            sums[0] = sums[0] + dot(gated, wq_v[0, ks])
            sums[1] = sums[1] + dot(gated, wq_v[1, ks])
            sums[2] = sums[2] + dot(gated, wkv_v[ks])
        total = jnp.sum(squares, axis=1, keepdims=True)
        for gg in range(2):
            part = slice(MB * gg, MB * gg + MB)
            s_out[m, gg] = jnp.broadcast_to(to_row(total[part]), (8, 128))
            for jj in range(2):
                q_out[m, 2 * gg + jj, :, 0:256] = sums[jj][part].astype(BF16)
                q_out[m, 2 * gg + jj, :, 256:512] = sums[2][part].astype(BF16)
        for k in range(1, NX):
            to = turn(k)
            remote(
                q_out.at[m, to], q_in.at[m, k - 1], q_s.at[m], q_r.at[m], at(to, y, z, c)
            ).start()
            remote(
                s_out.at[m, to // 2], s_in.at[m, k - 1], s_s.at[m], s_r.at[m], at(to, y, z, c)
            ).start()

    def attend(m):
        settle(s_in.at[m], s_r.at[m])
        settle(q_in.at[m], q_r.at[m])
        squares = s_out[m, x // 2] + s_in[m, 0] + s_in[m, 1] + s_in[m, 2]
        scale = lax.rsqrt(to_col(squares[0:1, 0:MB]) / D + EPS)
        qkv = q_out[m, x].astype(F32)
        for k in range(3):
            qkv = qkv + q_in[m, k].astype(F32)
        qkv = (qkv * scale).astype(BF16)
        query = jnp.concatenate([qkv[:, 0:128], qkv[:, 128:256]], axis=0)
        scores = dot_nt(query, qkv[:, 256:384]) * HD ** (-0.5)
        seg_row = seg[group, pl.ds(m, 1), :][:, 0:MB].astype(F32)
        allowed = (to_col(seg_row) == seg_row) & (iota((MB, MB), 1) <= iota((MB, MB), 0))
        top, low = scores[:MB], scores[MB:]
        halves = []
        for part in (top, low):
            part = jnp.where(allowed, part, -jnp.inf)
            weights = jnp.exp(part - jnp.max(part, axis=1, keepdims=True))
            halves.append((weights / jnp.sum(weights, axis=1, keepdims=True)).astype(BF16))
        for i in range(2):
            mx[m, :, 128 * i : 128 * i + 128] = dot(halves[i], qkv[:, 384:512]).astype(BF16)
        for dz in range(NZ):
            zz = (z + dz) % NZ
            if dz == 0:
                @pl.when(self_mx)
                def _():
                    local(mx.at[m], mixed.at[m, block], mx_r.at[m]).start()

                @pl.when(jnp.logical_not(self_mx))
                def _():
                    remote(
                        mx.at[m], mixed.at[m, block], mx_s.at[0, m], mx_r.at[m], at(ring, y, zz, c)
                    ).start()
            else:
                remote(
                    mx.at[m], mixed.at[m, block], mx_s.at[1, m], mx_r.at[m], at(ring, y, zz, c)
                ).start()

    def back(m):
        settle(mixed.at[m], mx_r.at[m])
        whole = [jnp.concatenate([mixed[m, j], mixed[m, 4 + j]], axis=0) for j in range(4)]
        for jj in range(2):
            sums = jnp.zeros((2 * MB, BLK), F32)
            for j in range(4):
                sums = sums + dot(whole[j], wo_v[jj, 256 * j : 256 * j + 256])
            for gg in range(2):
                kept = hid[m, 4 * gg + 2 * odd + jj].astype(F32)
                kept = jnp.where(x == ring, kept, 0.0)
                o_out[m, 2 * gg + jj] = (sums[MB * gg : MB * gg + MB] + kept).astype(BF16)
        for k in range(1, NX):
            to = turn(k)
            remote(
                o_out.at[m, to], o_in.at[m, k - 1], o_s.at[m], o_r.at[m], at(to, y, z, c)
            ).start()

    def forward(m):
        settle(o_in.at[m], o_r.at[m])
        new = o_out[m, x].astype(F32)
        for k in range(3):
            new = new + o_in[m, k].astype(F32)
        new = new.astype(BF16)

        @pl.when(y < 3)
        def _():
            h_out[M + m] = new
            for dz in range(NZ):
                remote(
                    h_out.at[M + m], hid.at[m, block], h_s.at[m], h_r.at[m],
                    at(ring, y + 1, (z + dz) % NZ, c),
                ).start()

        @pl.when(y == 3)
        def _():
            seg_row = seg[group, pl.ds(m, 1), :][:, 0:MB]
            hits = seg_row == iota((16, MB), 0)
            amount = jnp.maximum(jnp.sum(hits.astype(F32), axis=1, keepdims=True), 1.0)
            e_out[m] = (dot(hits.astype(BF16), new) / amount).astype(BF16)
            for k in range(NX):
                to = at(turn(k), m, z, x % 2)
                if k == 0:
                    is_self = (m == 3) & (x % 2 == c)

                    @pl.when(is_self)
                    def _():
                        local(e_out.at[m], e_in.at[group], e_r).start()

                    @pl.when(jnp.logical_not(is_self))
                    def _():
                        remote(e_out.at[m], e_in.at[group], e_s.at[0, m], e_r, to).start()
                else:
                    remote(e_out.at[m], e_in.at[group], e_s.at[1, m], e_r, to).start()

    def tick(i, carry):
        @pl.when(i < M)
        def _():
            project(i)

        @pl.when(i > 0)
        def _():
            back(i - 1)

        @pl.when(i < M)
        def _():
            attend(i)

        @pl.when(i > 0)
        def _():
            forward(i - 1)

        return carry

    lax.fori_loop(0, M + 1, tick, 0)

    settle(raw.at[0:3], x3_s.at[0])
    settle(seg.at[0:3], x3_s.at[1])
    settle(code.at[0:3], x3_s.at[2])
    settle(wq_v.at[0], one_s.at[0])
    settle(wo_v.at[0], one_s.at[1])
    settle(kvt.at[0:3], kv_s)

    @pl.when(jnp.logical_not(self_pro))
    def _():
        settle(h_out.at[0], pro_s.at[0])

    settle(hid.at[0, 0:7], pro_s.at[1])

    def drain(m, carry):
        settle(q_in.at[m], q_s.at[m])
        settle(s_in.at[m], s_s.at[m])
        settle(o_in.at[m], o_s.at[m])
        settle(mixed.at[m, 0:7], mx_s.at[1, m])

        @pl.when(jnp.logical_not(self_mx))
        def _():
            settle(mx.at[m], mx_s.at[0, m])

        @pl.when(y < 3)
        def _():
            settle(hid.at[m], h_s.at[m])

        @pl.when(y == 3)
        def _():
            settle(e_in.at[0:3], e_s.at[1, m])

            @pl.when(jnp.logical_not((m == 3) & (x % 2 == c)))
            def _():
                settle(e_in.at[0], e_s.at[0, m])

        return carry

    lax.fori_loop(0, M, drain, 0)

    settle(e_in, e_r)
    row = iota((16, 16), 0)
    col = iota((16, 16), 1)
    picked = jnp.zeros((16, BLK), F32)
    for g in range(NX):
        hits = ((row >> 1) & 3) == g
        hits = hits & ((row >= 8) == (col >= 3)) & (col < 6)
        hits = hits & (code[g, 0:1, 0:16] == 2 * x + (row & 1))
        picked = picked + dot(hits.astype(BF16), e_in[g])
    out[...] = picked.astype(BF16)


def shards(prompt_rows, row_dest, segment_ids, owner, gain, w_query, w_key, w_value, w_out):
    any_spec = pl.BlockSpec(memory_space=pl.ANY)
    vmem = pl.BlockSpec(memory_space=pltpu.VMEM)
    smem = pl.BlockSpec(memory_space=pltpu.SMEM)
    dma = pltpu.SemaphoreType.DMA
    embedded = pl.pallas_call(
        kernel,
        out_shape=jax.ShapeDtypeStruct((16, BLK), BF16),
        in_specs=[any_spec, vmem, vmem, smem, vmem, any_spec, any_spec, any_spec, any_spec],
        out_specs=vmem,
        scratch_shapes=[
            pltpu.VMEM((NX, MB, BLK), BF16),
            pltpu.VMEM((NX, 8, 128), I32),
            pltpu.VMEM((NX, 8, 128), I32),
            pltpu.VMEM((2, 2048, 256), BF16),
            pltpu.VMEM((2048, 32), BF16),
            pltpu.VMEM((2048, 32), BF16),
            pltpu.VMEM((4, 2, 32, 2048), BF16),
            pltpu.VMEM((2048, 256), BF16),
            pltpu.VMEM((2, 1024, BLK), BF16),
            pltpu.VMEM((M, 8, MB, BLK), BF16),
            pltpu.VMEM((M, 4, MB, BLK), BF16),
            pltpu.VMEM((M, 3, MB, BLK), BF16),
            pltpu.VMEM((M, 2, 8, 128), F32),
            pltpu.VMEM((M, 3, 8, 128), F32),
            pltpu.VMEM((M, MB, 256), BF16),
            pltpu.VMEM((M, 8, MB, 256), BF16),
            pltpu.VMEM((M, 4, MB, BLK), BF16),
            pltpu.VMEM((M, 3, MB, BLK), BF16),
            pltpu.VMEM((2 * M, MB, BLK), BF16),
            pltpu.VMEM((M, 16, BLK), BF16),
            pltpu.VMEM((NX, 16, BLK), BF16),
            dma((5,)),
            dma((2,)),
            dma((2,)),
            dma((3,)),
            dma((3,)),
            dma,
            dma,
            dma((2,)),
            dma((M,)),
            dma((M,)),
            dma((M,)),
            dma((M,)),
            dma((M,)),
            dma((2, M)),
            dma((M,)),
            dma((M,)),
            dma((M,)),
            dma((M,)),
            dma((2, M)),
            dma,
        ],
        compiler_params=pltpu.CompilerParams(
            collective_id=0, has_side_effects=True, vmem_limit_bytes=48 << 20
        ),
        name="sections",
    )(
        prompt_rows.reshape(MB, BLK),
        row_dest,
        segment_ids,
        owner.reshape(2, 3),
        gain,
        w_query[0],
        w_key[0],
        w_value[0],
        w_out[0],
    )
    return embedded.reshape(1, 2, 8, BLK)


def solution(mesh):
    in_specs = (
        P("dp", "phase", None, "mp"),
        P(None, "phase", None),
        P("dp", None, None),
        P("dp", "phase", None, None),
        P("phase", None),
        P("phase", "dp", "mp"),
        P("phase", "dp", "mp"),
        P("phase", "dp", "mp"),
        P("phase", "dp", "mp"),
    )
    out_specs = P("dp", "phase", None, "mp")
    return jax.shard_map(shards, mesh=mesh, in_specs=in_specs, out_specs=out_specs, check_vma=False)
```

time: 749 us -> 205 us (0.27); the launches traced: 740 us -> 204 us
  blocking collectives: 559 us -> 0 us
  Pallas kernels: 0 us -> 199 us
  waiting for transfers between devices: 65.5 us -> 0 us
  matrix products: 36.4 us -> 0 us
  local copies, waits for them, and re-layouts: 37.2 us -> 4.95 us
  other arithmetic: 14.2 us -> 0 us
  between operations: 13.6 us -> 0.1 us
  starting transfers between devices: 13.1 us -> 0 us
    all_gather x31 -> x0, blocking collectives: 541 us -> none  [the longest x7 131 us: advance(): whole_rows = lax.all_gather(tok_rows, 'mp', axis=1, tiled=True)]
    pallas_call x0 -> x1, Pallas kernels: none -> 199 us  [shards(): pl.pallas_call(kernel, out_shape=jax.ShapeDtypeStruct((16, BLK), BF16), i...]
    ppermute x7 -> x0, waiting for transfers between devices: 44.1 us -> none  [from_behind(): lax.ppermute(value, axis, [(source, source + steps) for source in range(i...]
    cond x4 -> x0, matrix products: 20.6 us -> none  [advance(): lax.cond(active, lambda: jnp.dot((whole_float * gain_row[None, :]).astype...]
    all_gather x2 -> x0, waiting for transfers between devices: 20 us -> none  [the longest x1 20 us: shards(): lax.all_gather(w_out[0], 'dp', axis=0, tiled=True)]
    scatter x5 -> x0, local copies, waits for them, and re-layouts: 17.4 us -> none  [the longest x1 11.3 us: shards(): own_halves = jnp.zeros((halves_here, half_rows, feature_cols), jnp.bfloat...]
    dot_general x25 -> x0, matrix products: 15.7 us -> none  [the longest x4 12 us: advance(): jnp.dot(mixed, back_rows, preferred_element_type=jnp.float32)]
    psum x1 -> x0, blocking collectives: 10.6 us -> none  [broadcast(): return lax.psum(jnp.where(mine, value, jnp.zeros_like(value)), axis)]
  transfers between devices with their start and end apart: 10 -> 0, of which waited for: 8 -> 0; matrix products, arithmetic and copies ran while one was open for 4% -> 0% of each run, Pallas kernels for 0% -> 0%
where the time goes in v1:
time: 205 us; the launch traced here: 204 us
  Pallas kernels  199 us (97%)
  local copies, waits for them, and re-layouts  4.95 us (2%)
    pallas_call x1, Pallas kernels, shards(): pl.pallas_call(kernel, out_shape=jax.ShapeDtypeStruct((16, BLK), BF16), i...  199 us
    unnamed x17, local copies, waits for them, and re-layouts  4.95 us

profile of v1, /device:TPU:25, one launch (start us, length us, event | category | flops | bytes accessed | tf_op | source)
XLA Modules:
  0.0 204.4 jit_solution(2152803146972010176)
XLA Ops:
  0.0 0.0 copy-start
  0.0 1.3 copy.10
  1.3 0.0 copy-start.2
  1.3 0.0 copy-start.3
  1.3 0.0 copy-start.4
  1.3 0.0 copy-start.5
  1.3 1.2 copy.11
  2.5 0.0 copy-start.6
  2.5 0.0 copy-done
  2.5 0.0 copy-done.2
  2.6 0.0 copy-done.3
  2.6 0.0 copy-done.4
  2.6 0.0 copy-done.5
  2.6 0.6 copy-done.6
  3.2 0.0 copy-start.1
  3.2 1.2 copy-done.1
  4.4 199.4 %sections.1 = bf16[16,512]{1,0:T(8,128)(2,1)S(1)} custom-call(bf16[48,512]{1,0:T(8,128)(2,1)S(1)} %bitcast.12, s32[4,2,24]{2,1,0:T(2,128)S(1)} %copy-done.4, s32[1,4,48]{2,1,0:T(4,128)S(1)} %copy-done.5, s32[2,3]{1,0:T(2,128)S(1)} %bitcast.13, f32[1,8192]{1,0:T(1,128)S(1)} %copy-done.3, bf16[2048,256]{1,0:T(8,128)(2,1)S(1)} %bitcast.9, ...), custom_call_target="tpu_custom_call" | custom-call | tf_op jit(solution)/shard_map/sections/pallas_call | solution.py:415
  203.8 0.6 copy.13
Async XLA Ops:
  0.0 2.5 %copy-start = (bf16[1,2048,256]{2,1,0:T(8,128)(2,1)S(1)}, bf16[1,2048,256]{2,1,0:T(8,128)(2,1)}, u32[]{:S(2)}) copy-start(bf16[1,2048,256]{2,1,0:T(8,128)(2,1)} %param.14) | copy-start | bytes 3145732
  1.3 1.3 copy-start.2
  1.3 1.3 copy-start.3
  1.3 1.3 copy-start.4
  1.3 1.3 copy-start.5
  2.5 0.7 copy-start.6
  3.2 1.2 copy-start.1

commit v2 on v1

v2 whole, which is shorter than its diff:
```python
import jax
import jax.numpy as jnp
from jax import lax
from jax.experimental import pallas as pl
from jax.experimental.pallas import tpu as pltpu
from jax.sharding import PartitionSpec as P

MESH = pl.DeviceIdType.MESH
F32 = jnp.float32
BF16 = jnp.bfloat16
I32 = jnp.int32

D = 8192
HD = 128
MB = 48
M = 4
NX = 4
NZ = 8
EPS = 1e-05
BLK = 512
T = 2 * M
FAR = (4, 3, 5, 2, 6, 1, 7)


def iota(shape, dim):
    return lax.broadcasted_iota(I32, shape, dim)


def dot(a, b):
    return jnp.dot(a, b, preferred_element_type=F32)


def dot_nt(a, b):
    return lax.dot_general(a, b, (((1,), (1,)), ((), ())), preferred_element_type=F32)


def to_row(col):
    eye = iota((MB, 128), 0) == iota((MB, 128), 1)
    return jnp.sum(jnp.where(eye, col, 0.0), axis=0, keepdims=True)


def to_col(row):
    eye = iota((MB, MB), 0) == iota((MB, MB), 1)
    return jnp.sum(jnp.where(eye, row, 0.0), axis=1, keepdims=True)


def kernel(
    rows, row_dest, segs, owner, gain, wq, wk, wv, wo, out,
    raw, seg, code, wq_v, kvt, wkv_v, wo_v, packed,
    hid, q_out, q_in, s_out, s_in, mx, mixed, o_out, o_in, h_out, e_out, e_in,
    loc, one_s, one_r, x3_s, x3_r, kv_s, kv_r, pro_s, h_r,
    q_s, q_r, s_s, s_r, mx_s, mx_r, o_s, o_r, h_s, e_s, e_r, go,
):
    x = lax.axis_index("dp")
    y = lax.axis_index("phase")
    p = lax.axis_index("mp")
    z = p // 2
    c = p % 2
    ring = z // 2
    odd = z % 2

    def at(xx, yy, zz, cc):
        return (xx, yy, zz * 2 + cc)

    def remote(src, dst, send, recv, device):
        return pltpu.make_async_remote_copy(
            src_ref=src, dst_ref=dst, send_sem=send, recv_sem=recv,
            device_id=device, device_id_type=MESH,
        )

    def local(src, dst, sem):
        return pltpu.make_async_copy(src, dst, sem)

    def settle(ref, sem):
        pltpu.make_async_copy(ref, ref, sem).wait()

    def turn(k):
        return (x + k) % NX

    quad = 2 * odd + c
    loads = [
        local(rows, raw.at[x], loc.at[0]),
        local(wk, kvt.at[quad, 0], loc.at[1]),
        local(wv, kvt.at[quad, 1], loc.at[2]),
        local(wq, wq_v.at[c], loc.at[3]),
        local(wo, wo_v.at[c], loc.at[4]),
    ]
    for load in loads:
        load.start()

    barrier = pltpu.get_barrier_semaphore()

    def greet(device):
        pl.semaphore_signal(barrier, inc=1, device_id=device, device_id_type=MESH)

    pair_z = z + 1 - 2 * odd
    self_mx = x == ring
    self_pro = (y == 0) & (x == ring) & (c == x // 2)
    self_e = (y == 3) & (x // 2 == c)
    greet(at(x, y, z, 1 - c))
    greet(at(x, y, pair_z, c))
    for k in range(1, NX):
        greet(at(turn(k), y, z, c))
    for r in range(NX):
        for e in range(2):
            @pl.when(jnp.logical_not((x == r) & (2 * x + e == z)))
            def _():
                greet(at(r, y, 2 * x + e, c))

    @pl.when(y > 0)
    def _():
        greet(at(x, 0, z, c))
        for r in range(NX):
            for e in range(2):
                greet(at(r, y - 1, 2 * x + e, c))

    @pl.when(y == 0)
    def _():
        for f in range(M):
            for gg in range(2):
                for e in range(2):
                    for cc in range(2):
                        if f == 0:
                            @pl.when(jnp.logical_not((2 * c + gg == x) & (2 * x + e == z) & (c == cc)))
                            def _():
                                greet(at(2 * c + gg, f, 2 * x + e, cc))
                        else:
                            greet(at(2 * c + gg, f, 2 * x + e, cc))

    for b in range(2):
        for cc in range(2):
            @pl.when(jnp.logical_not((y == 3) & (2 * c + b == x) & (c == cc)))
            def _():
                greet(at(2 * c + b, 3, z, cc))

    seg[x] = jnp.zeros((8, 128), I32)
    seg[x, 0:4, 0:MB] = segs[0]
    lane = iota((8, 128), 1)
    table = jnp.full((8, 128), -1, I32)
    for t in range(2):
        for i in range(3):
            who = owner[t, i]
            rank = jnp.int32(0)
            for before in range(i):
                rank = rank + (owner[t, before] == who).astype(I32)
            table = jnp.where(lane == 3 * t + i, 2 * who + rank, table)
    code[x] = table

    count = 21 + jnp.where(y == 0, 3, 0) - self_mx.astype(I32) - self_pro.astype(I32)
    count = count + jnp.where(y < 3, 8, 16) - self_e.astype(I32)
    pl.semaphore_wait(barrier, count)

    def start_pairs():
        loads[1].wait()
        loads[2].wait()
        mine = kvt.at[quad]
        remote(mine, mine, kv_s.at[0], kv_r.at[0], at(x, y, pair_z, c)).start()
        remote(mine, mine, kv_s.at[1], kv_r.at[1], at(x, y, z, 1 - c)).start()

    def start_core():
        loads[3].wait()
        remote(wq_v.at[c], wq_v.at[c], one_s.at[0], one_r.at[0], at(x, y, z, 1 - c)).start()
        loads[4].wait()
        remote(wo_v.at[c], wo_v.at[c], one_s.at[1], one_r.at[1], at(x, y, z, 1 - c)).start()

    loads[0].wait()
    for k in (2, 1, 3):
        remote(raw.at[x], raw.at[x], x3_s.at[0], x3_r.at[0], at(turn(k), y, z, c)).start()
    start_pairs()
    for k in range(1, NX):
        remote(seg.at[x], seg.at[x], x3_s.at[1], x3_r.at[1], at(turn(k), y, z, c)).start()
        remote(code.at[x], code.at[x], x3_s.at[2], x3_r.at[2], at(turn(k), y, z, c)).start()
    start_core()

    settle(raw.at[0:3], x3_r.at[0])
    dest = row_dest[...].astype(F32)
    spread = [
        (iota((24, MB), 0) + 24 * t == iota((24, MB), 1)).astype(F32) for t in range(2)
    ]
    dest = dot(dest[:, 0, :], spread[0]) + dot(dest[:, 1, :], spread[1])
    slot = iota((MB, MB), 0)
    place = iota((MB, MB), 1)
    upper = slot >= 24
    wanted = (slot - jnp.where(upper, 24, 0) + 24 * x).astype(F32)
    same_half = upper == (place >= 24)
    order = jnp.zeros((MB, BLK), F32)
    for l in range(NX):
        hits = same_half & (dest[l : l + 1, :] == wanted)
        order = order + dot(hits.astype(BF16), raw[l])
    packed[...] = order.astype(BF16)
    step = 2 * y + x % 2
    first = hid.at[step, quad]

    @pl.when(y > 0)
    def _():
        pl.semaphore_wait(go, 1)

    for dz in FAR:
        remote(
            packed, first, pro_s.at[1], h_r.at[step], at(ring, 0, (z + dz) % NZ, x // 2)
        ).start()

    @pl.when(self_pro)
    def _():
        local(packed, first, h_r.at[step]).start()

    @pl.when(jnp.logical_not(self_pro))
    def _():
        remote(packed, first, pro_s.at[0], h_r.at[step], at(ring, 0, z, x // 2)).start()

    settle(kvt.at[0], kv_r.at[0])
    other = kvt.at[2 - 2 * odd + c]
    remote(other, other, kv_s.at[2], kv_r.at[2], at(x, y, z, 1 - c)).start()
    settle(kvt.at[0], kv_r.at[1])
    settle(kvt.at[0], kv_r.at[2])
    for t in range(2):
        wkv_v[:, 128 * t : 128 * t + 128] = jnp.concatenate(
            [kvt[j, t] for j in range(4)], axis=0
        ).T
    settle(wq_v.at[0], one_r.at[0])
    settle(wo_v.at[0], one_r.at[1])
    settle(seg.at[0:3], x3_r.at[1])
    settle(code.at[0:3], x3_r.at[2])

    def project(t):
        settle(hid.at[t], h_r.at[t])
        squares = jnp.zeros((MB, 128), F32)
        sums = [jnp.zeros((MB, 256), F32) for _ in range(3)]
        for j in range(4):
            h = hid[t, j].astype(F32)
            square = h * h
            for i in range(4):
                squares = squares + square[:, 128 * i : 128 * i + 128]
            g = gain[:, pl.ds(pl.multiple_of(x * 2048 + BLK * j, BLK), BLK)]
            gated = (h * g).astype(BF16)
            ks = slice(BLK * j, BLK * j + BLK)
            sums[0] = sums[0] + dot(gated, wq_v[0, ks])
            sums[1] = sums[1] + dot(gated, wq_v[1, ks])
            sums[2] = sums[2] + dot(gated, wkv_v[ks])
        total = jnp.sum(squares, axis=1, keepdims=True)
        s_out[t] = jnp.broadcast_to(to_row(total), (8, 128))
        for r in range(NX):
            q_out[t, r, :, 0:128] = sums[r // 2][:, 128 * (r % 2) : 128 * (r % 2) + 128].astype(BF16)
            q_out[t, r, :, 128:384] = sums[2].astype(BF16)
        for k in (2, 1, 3):
            to = turn(k)
            remote(
                q_out.at[t, to], q_in.at[t, k - 1], q_s.at[t], q_r.at[t], at(to, y, z, c)
            ).start()
            remote(
                s_out.at[t], s_in.at[t, k - 1], s_s.at[t], s_r.at[t], at(to, y, z, c)
            ).start()

    def attend(t):
        settle(s_in.at[t], s_r.at[t])
        settle(q_in.at[t], q_r.at[t])
        squares = s_out[t] + s_in[t, 0] + s_in[t, 1] + s_in[t, 2]
        scale = lax.rsqrt(to_col(squares[0:1, 0:MB]) / D + EPS)
        qkv = q_out[t, x].astype(F32)
        for k in range(3):
            qkv = qkv + q_in[t, k].astype(F32)
        qkv = (qkv * scale).astype(BF16)
        scores = dot_nt(qkv[:, 0:128], qkv[:, 128:256]) * HD ** (-0.5)
        seg_row = seg[2 * c + t % 2, pl.ds(t // 2, 1), :][:, 0:MB].astype(F32)
        allowed = (to_col(seg_row) == seg_row) & (iota((MB, MB), 1) <= iota((MB, MB), 0))
        scores = jnp.where(allowed, scores, -jnp.inf)
        weights = jnp.exp(scores - jnp.max(scores, axis=1, keepdims=True))
        probs = (weights / jnp.sum(weights, axis=1, keepdims=True)).astype(BF16)
        mx[t] = dot(probs, qkv[:, 256:384]).astype(BF16)
        place = mixed.at[t, 4 * odd + x]
        for dz in FAR:
            remote(
                mx.at[t], place, mx_s.at[1, t], mx_r.at[t], at(ring, y, (z + dz) % NZ, c)
            ).start()

        @pl.when(self_mx)
        def _():
            local(mx.at[t], place, mx_r.at[t]).start()

        @pl.when(jnp.logical_not(self_mx))
        def _():
            remote(mx.at[t], place, mx_s.at[0, t], mx_r.at[t], at(ring, y, z, c)).start()

    def back(t):
        settle(mixed.at[t], mx_r.at[t])
        whole = jnp.concatenate([mixed[t, j] for j in range(8)], axis=1)
        for jj in range(2):
            sums = dot(whole, wo_v[jj])
            kept = hid[t, 2 * odd + jj].astype(F32)
            sums = (sums + jnp.where(x == ring, kept, 0.0)).astype(BF16)
            for i in range(2):
                o_out[t, 2 * jj + i] = sums[:, 256 * i : 256 * i + 256]
        for k in (2, 1, 3):
            to = turn(k)
            remote(
                o_out.at[t, to], o_in.at[t, k - 1], o_s.at[t], o_r.at[t], at(to, y, z, c)
            ).start()

    def forward(t):
        settle(o_in.at[t], o_r.at[t])
        new = o_out[t, x].astype(F32)
        for k in range(3):
            new = new + o_in[t, k].astype(F32)
        new = new.astype(BF16)

        @pl.when(y < 3)
        def _():
            h_out[t] = new
            lanes = pl.ds(pl.multiple_of(256 * (x % 2), 256), 256)
            for dz in FAR + (0,):
                remote(
                    h_out.at[t], hid.at[t, 2 * odd + x // 2, :, lanes], h_s.at[t], h_r.at[t],
                    at(ring, y + 1, (z + dz) % NZ, c),
                ).start()

        @pl.when(y == 3)
        def _():
            group = 2 * c + t % 2
            seg_row = seg[group, pl.ds(t // 2, 1), :][:, 0:MB]
            hits = seg_row == iota((16, MB), 0)
            amount = jnp.maximum(jnp.sum(hits.astype(F32), axis=1, keepdims=True), 1.0)
            e_out[t] = (dot(hits.astype(BF16), new) / amount).astype(BF16)
            place = e_in.at[x % 2, group]
            for k in (2, 1, 3):
                remote(
                    e_out.at[t], place, e_s.at[1, t], e_r, at(turn(k), t // 2, z, x // 2)
                ).start()
            is_self = (t // 2 == 3) & (x // 2 == c)

            @pl.when(is_self)
            def _():
                local(e_out.at[t], place, e_r).start()

            @pl.when(jnp.logical_not(is_self))
            def _():
                remote(e_out.at[t], place, e_s.at[0, t], e_r, at(x, t // 2, z, x // 2)).start()

    def tick(i, carry):
        @pl.when(i < T)
        def _():
            project(i)

        @pl.when((y == 0) & (i < T - 2) & (i % 2 == 0))
        def _():
            pl.semaphore_signal(
                go, inc=1, device_id=at(x, i // 2 + 1, z, c), device_id_type=MESH
            )

        @pl.when(i > 1)
        def _():
            forward(i - 2)

        @pl.when(i < T)
        def _():
            attend(i)

        @pl.when((i > 0) & (i <= T))
        def _():
            back(i - 1)

        return carry

    lax.fori_loop(0, T + 2, tick, 0)

    settle(raw.at[0:3], x3_s.at[0])
    settle(seg.at[0:3], x3_s.at[1])
    settle(code.at[0:3], x3_s.at[2])
    settle(wq_v.at[0], one_s.at[0])
    settle(wo_v.at[0], one_s.at[1])
    for k in range(3):
        settle(kvt.at[0], kv_s.at[k])

    @pl.when(jnp.logical_not(self_pro))
    def _():
        settle(packed, pro_s.at[0])

    settle(hid.at[0], pro_s.at[1])
    settle(hid.at[0, 0:3], pro_s.at[1])

    def drain(t, carry):
        settle(q_in.at[t], q_s.at[t])
        settle(s_in.at[t], s_s.at[t])
        settle(o_in.at[t], o_s.at[t])
        settle(mixed.at[t, 0:7], mx_s.at[1, t])

        @pl.when(jnp.logical_not(self_mx))
        def _():
            settle(mx.at[t], mx_s.at[0, t])

        @pl.when(y < 3)
        def _():
            settle(hid.at[t], h_s.at[t])

        @pl.when(y == 3)
        def _():
            settle(e_in.at[0, 0:3], e_s.at[1, t])

            @pl.when(jnp.logical_not((t // 2 == 3) & (x // 2 == c)))
            def _():
                settle(e_in.at[0, 0], e_s.at[0, t])

        return carry

    lax.fori_loop(0, T, drain, 0)

    settle(e_in, e_r)
    row = iota((16, 16), 0)
    col = iota((16, 16), 1)
    picked = [jnp.zeros((16, 256), F32) for _ in range(2)]
    for g in range(NX):
        hits = ((row >> 1) & 3) == g
        hits = hits & ((row >= 8) == (col >= 3)) & (col < 6)
        hits = (hits & (code[g, 0:1, 0:16] == 2 * x + (row & 1))).astype(BF16)
        for i in range(2):
            picked[i] = picked[i] + dot(hits, e_in[i, g])
    for i in range(2):
        out[:, 256 * i : 256 * i + 256] = picked[i].astype(BF16)


def shards(prompt_rows, row_dest, segment_ids, owner, gain, w_query, w_key, w_value, w_out):
    any_spec = pl.BlockSpec(memory_space=pl.ANY)
    vmem = pl.BlockSpec(memory_space=pltpu.VMEM)
    smem = pl.BlockSpec(memory_space=pltpu.SMEM)
    dma = pltpu.SemaphoreType.DMA
    embedded = pl.pallas_call(
        kernel,
        out_shape=jax.ShapeDtypeStruct((16, BLK), BF16),
        in_specs=[any_spec, vmem, vmem, smem, vmem, any_spec, any_spec, any_spec, any_spec],
        out_specs=vmem,
        scratch_shapes=[
            pltpu.VMEM((NX, MB, BLK), BF16),
            pltpu.VMEM((NX, 8, 128), I32),
            pltpu.VMEM((NX, 8, 128), I32),
            pltpu.VMEM((2, 2048, 256), BF16),
            pltpu.VMEM((4, 2, 32, 2048), BF16),
            pltpu.VMEM((2048, 256), BF16),
            pltpu.VMEM((2, 1024, BLK), BF16),
            pltpu.VMEM((MB, BLK), BF16),
            pltpu.VMEM((T, 4, MB, BLK), BF16),
            pltpu.VMEM((T, 4, MB, 384), BF16),
            pltpu.VMEM((T, 3, MB, 384), BF16),
            pltpu.VMEM((T, 8, 128), F32),
            pltpu.VMEM((T, 3, 8, 128), F32),
            pltpu.VMEM((T, MB, 128), BF16),
            pltpu.VMEM((T, 8, MB, 128), BF16),
            pltpu.VMEM((T, 4, MB, 256), BF16),
            pltpu.VMEM((T, 3, MB, 256), BF16),
            pltpu.VMEM((T, MB, 256), BF16),
            pltpu.VMEM((T, 16, 256), BF16),
            pltpu.VMEM((2, NX, 16, 256), BF16),
            dma((5,)),
            dma((2,)),
            dma((2,)),
            dma((3,)),
            dma((3,)),
            dma((3,)),
            dma((3,)),
            dma((2,)),
            dma((T,)),
            dma((T,)),
            dma((T,)),
            dma((T,)),
            dma((T,)),
            dma((2, T)),
            dma((T,)),
            dma((T,)),
            dma((T,)),
            dma((T,)),
            dma((2, T)),
            dma,
            pltpu.SemaphoreType.REGULAR,
        ],
        compiler_params=pltpu.CompilerParams(
            collective_id=0, has_side_effects=True, vmem_limit_bytes=60 << 20
        ),
        name="sections",
    )(
        prompt_rows.reshape(MB, BLK),
        row_dest,
        segment_ids,
        owner.reshape(2, 3),
        gain,
        w_query[0],
        w_key[0].T,
        w_value[0].T,
        w_out[0],
    )
    return embedded.reshape(1, 2, 8, BLK)


def solution(mesh):
    in_specs = (
        P("dp", "phase", None, "mp"),
        P(None, "phase", None),
        P("dp", None, None),
        P("dp", "phase", None, None),
        P("phase", None),
        P("phase", "dp", "mp"),
        P("phase", "dp", "mp"),
        P("phase", "dp", "mp"),
        P("phase", "dp", "mp"),
    )
    out_specs = P("dp", "phase", None, "mp")
    return jax.shard_map(shards, mesh=mesh, in_specs=in_specs, out_specs=out_specs, check_vma=False)
```

time: 205 us -> 180 us (0.88)
  Pallas kernels: 199 us -> 178 us
  local copies, waits for them, and re-layouts: 4.95 us -> 1.32 us
    pallas_call x1, Pallas kernels: 199 us -> 178 us  [shards(): pl.pallas_call(kernel, out_shape=jax.ShapeDtypeStruct((16, BLK), BF16), i...]
    unnamed x17 -> x1, local copies, waits for them, and re-layouts: 4.95 us -> 1.32 us
where the time goes in v2:
time: 180 us
  Pallas kernels  178 us (99%)
    pallas_call x1, Pallas kernels, shards(): pl.pallas_call(kernel, out_shape=jax.ShapeDtypeStruct((16, BLK), BF16), i...  178 us

profile of v2, /device:TPU:25, one launch (start us, length us, event | category | flops | bytes accessed | tf_op | source)
XLA Modules:
  0.0 179.5 jit_solution(2698723600151428359)
XLA Ops:
  0.0 178.2 %sections.1 = bf16[16,512]{1,0:T(8,128)(2,1)} custom-call(bf16[48,512]{1,0:T(8,128)(2,1)} %bitcast.16, s32[4,2,24]{2,1,0:T(2,128)} %row_dest.1, s32[1,4,48]{2,1,0:T(4,128)} %segs.1, s32[2,3]{1,0:T(2,128)} %bitcast.17, f32[1,8192]{1,0:T(1,128)} %gain.1, bf16[2048,256]{1,0:T(8,128)(2,1)} %bitcast.11, bf16[32,2048]{1,0:T(8,128)(2,1)} %bitcast.13, ...), custom_call_target="tpu_custom_call" | custom-call | tf_op jit(solution)/shard_map/sections/pallas_call | solution.py:425
  178.2 1.3 copy.11

commit v3 on v2

--- a/solution.py
+++ b/solution.py
@@ -21,6 +21,13 @@
 T = 2 * M
 FAR = (4, 3, 5, 2, 6, 1, 7)
 
+ORDERS = (
+    "PPAPABPABFPABFPABFPABFPABFABFBFF",
+    "PAPABPFABPFABPFABPFBPAFPABABFBFF",
+    "PAPABPFABPFABPFABPFBPAFPABABFBFF",
+    "PAPABPFABPFABPFABPFBPAFPABABFBFF",
+)
+
 
 def iota(shape, dim):
     return lax.broadcasted_iota(I32, shape, dim)
@@ -46,10 +53,10 @@
 
 def kernel(
     rows, row_dest, segs, owner, gain, wq, wk, wv, wo, out,
-    raw, seg, code, wq_v, kvt, wkv_v, wo_v, packed,
+    raw, seg, code, wq_v, kvt, wkv_v, wo_v, packed, staged,
     hid, q_out, q_in, s_out, s_in, mx, mixed, o_out, o_in, h_out, e_out, e_in,
     loc, one_s, one_r, x3_s, x3_r, kv_s, kv_r, pro_s, h_r,
-    q_s, q_r, s_s, s_r, mx_s, mx_r, o_s, o_r, h_s, e_s, e_r, go,
+    q_s, q_r, s_s, s_r, mx_s, mx_r, o_s, o_r, h_s, e_s, e_r, go, st_s, st_r,
 ):
     x = lax.axis_index("dp")
     y = lax.axis_index("phase")
@@ -78,8 +85,12 @@
         return (x + k) % NX
 
     quad = 2 * odd + c
+
+    def half_of(k):
+        return pl.ds(pl.multiple_of(256 * (k % 2), 256), 256)
+
     loads = [
-        local(rows, raw.at[x], loc.at[0]),
+        local(rows.at[:, half_of(x)], raw.at[x], loc.at[0]),
         local(wk, kvt.at[quad, 0], loc.at[1]),
         local(wv, kvt.at[quad, 1], loc.at[2]),
         local(wq, wq_v.at[c], loc.at[3]),
@@ -97,6 +108,9 @@
     self_mx = x == ring
     self_pro = (y == 0) & (x == ring) & (c == x // 2)
     self_e = (y == 3) & (x // 2 == c)
+    from_x, from_z, from_c = 2 * c + z % 2, 2 * x + z // 4, (z // 2) % 2
+    self_st = (from_x == x) & (from_z == z) & (from_c == c)
+    to_z = 4 * odd + 2 * c + x % 2
     greet(at(x, y, z, 1 - c))
     greet(at(x, y, pair_z, c))
     for k in range(1, NX):
@@ -116,16 +130,19 @@
 
     @pl.when(y == 0)
     def _():
-        for f in range(M):
-            for gg in range(2):
-                for e in range(2):
-                    for cc in range(2):
-                        if f == 0:
-                            @pl.when(jnp.logical_not((2 * c + gg == x) & (2 * x + e == z) & (c == cc)))
-                            def _():
-                                greet(at(2 * c + gg, f, 2 * x + e, cc))
-                        else:
-                            greet(at(2 * c + gg, f, 2 * x + e, cc))
+        for gg in range(2):
+            for e in range(2):
+                for cc in range(2):
+                    @pl.when(jnp.logical_not((2 * c + gg == x) & (2 * x + e == z) & (c == cc)))
+                    def _():
+                        greet(at(2 * c + gg, 0, 2 * x + e, cc))
+        for f in range(1, M):
+            for zz in range(NZ):
+                greet(at(x, f, zz, c))
+
+    @pl.when((y > 0) & jnp.logical_not(self_st))
+    def _():
+        greet(at(from_x, y, from_z, from_c))
 
     for b in range(2):
         for cc in range(2):
@@ -146,7 +163,7 @@
             table = jnp.where(lane == 3 * t + i, 2 * who + rank, table)
     code[x] = table
 
-    count = 21 + jnp.where(y == 0, 3, 0) - self_mx.astype(I32) - self_pro.astype(I32)
+    count = 21 + jnp.where(y == 0, 3, jnp.where(self_st, 0, 1)) - self_mx.astype(I32) - self_pro.astype(I32)
     count = count + jnp.where(y < 3, 8, 16) - self_e.astype(I32)
     pl.semaphore_wait(barrier, count)
 
@@ -163,16 +180,17 @@
         loads[4].wait()
         remote(wo_v.at[c], wo_v.at[c], one_s.at[1], one_r.at[1], at(x, y, z, 1 - c)).start()
 
-    loads[0].wait()
     for k in (2, 1, 3):
-        remote(raw.at[x], raw.at[x], x3_s.at[0], x3_r.at[0], at(turn(k), y, z, c)).start()
+        to = turn(k)
+        remote(
+            rows.at[:, half_of(to)], raw.at[x], x3_s.at[0], x3_r.at[0], at(to, y, z, c)
+        ).start()
     start_pairs()
     for k in range(1, NX):
         remote(seg.at[x], seg.at[x], x3_s.at[1], x3_r.at[1], at(turn(k), y, z, c)).start()
         remote(code.at[x], code.at[x], x3_s.at[2], x3_r.at[2], at(turn(k), y, z, c)).start()
     start_core()
 
-    settle(raw.at[0:3], x3_r.at[0])
     dest = row_dest[...].astype(F32)
     spread = [
         (iota((24, MB), 0) + 24 * t == iota((24, MB), 1)).astype(F32) for t in range(2)
@@ -181,32 +199,47 @@
     slot = iota((MB, MB), 0)
     place = iota((MB, MB), 1)
     upper = slot >= 24
-    wanted = (slot - jnp.where(upper, 24, 0) + 24 * x).astype(F32)
+    slot = slot - jnp.where(upper, 24, 0)
     same_half = upper == (place >= 24)
-    order = jnp.zeros((MB, BLK), F32)
-    for l in range(NX):
-        hits = same_half & (dest[l : l + 1, :] == wanted)
-        order = order + dot(hits.astype(BF16), raw[l])
-    packed[...] = order.astype(BF16)
-    step = 2 * y + x % 2
-    first = hid.at[step, quad]
-
-    @pl.when(y > 0)
-    def _():
-        pl.semaphore_wait(go, 1)
-
-    for dz in FAR:
-        remote(
-            packed, first, pro_s.at[1], h_r.at[step], at(ring, 0, (z + dz) % NZ, x // 2)
-        ).start()
-
-    @pl.when(self_pro)
-    def _():
-        local(packed, first, h_r.at[step]).start()
-
-    @pl.when(jnp.logical_not(self_pro))
-    def _():
-        remote(packed, first, pro_s.at[0], h_r.at[step], at(ring, 0, z, x // 2)).start()
+    loads[0].wait()
+    settle(raw.at[0:3], x3_r.at[0])
+
+    for h in range(2):
+        wanted = (slot + 24 * (h + 2 * (x // 2))).astype(F32)
+        order = jnp.zeros((MB, 256), F32)
+        for l in range(NX):
+            hits = same_half & (dest[l : l + 1, :] == wanted)
+            order = order + dot(hits.astype(BF16), raw[l])
+        packed[h] = order.astype(BF16)
+
+        @pl.when(y == 0)
+        def _():
+            first = hid.at[h, quad, :, half_of(x)]
+            for dz in FAR:
+                remote(
+                    packed.at[h], first, pro_s.at[1, h], h_r.at[h],
+                    at(ring, 0, (z + dz) % NZ, x // 2),
+                ).start()
+
+            @pl.when(self_pro)
+            def _():
+                local(packed.at[h], first, h_r.at[h]).start()
+
+            @pl.when(jnp.logical_not(self_pro))
+            def _():
+                remote(
+                    packed.at[h], first, pro_s.at[0, h], h_r.at[h], at(ring, 0, z, x // 2)
+                ).start()
+
+        @pl.when((y > 0) & self_st)
+        def _():
+            local(packed.at[h], staged.at[h], st_r).start()
+
+        @pl.when((y > 0) & jnp.logical_not(self_st))
+        def _():
+            remote(
+                packed.at[h], staged.at[h], st_s.at[h], st_r, at(ring, y, to_z, x // 2)
+            ).start()
 
     settle(kvt.at[0], kv_r.at[0])
     other = kvt.at[2 - 2 * odd + c]
@@ -219,6 +252,19 @@
         ).T
     settle(wq_v.at[0], one_r.at[0])
     settle(wo_v.at[0], one_r.at[1])
+
+    @pl.when(y > 0)
+    def _():
+        settle(staged, st_r)
+        pl.semaphore_wait(go, 1)
+        for h in range(2):
+            first = hid.at[2 * y + h, 2 * (z // 4) + (z // 2) % 2, :, half_of(z)]
+            for dz in FAR + (0,):
+                remote(
+                    staged.at[h], first, pro_s.at[1, h], h_r.at[2 * y + h],
+                    at(x, 0, (z + dz) % NZ, c),
+                ).start()
+
     settle(seg.at[0:3], x3_r.at[1])
     settle(code.at[0:3], x3_r.at[2])
 
@@ -306,10 +352,9 @@
         @pl.when(y < 3)
         def _():
             h_out[t] = new
-            lanes = pl.ds(pl.multiple_of(256 * (x % 2), 256), 256)
             for dz in FAR + (0,):
                 remote(
-                    h_out.at[t], hid.at[t, 2 * odd + x // 2, :, lanes], h_s.at[t], h_r.at[t],
+                    h_out.at[t], hid.at[t, 2 * odd + x // 2, :, half_of(x)], h_s.at[t], h_r.at[t],
                     at(ring, y + 1, (z + dz) % NZ, c),
                 ).start()
 
@@ -335,32 +380,37 @@
             def _():
                 remote(e_out.at[t], place, e_s.at[0, t], e_r, at(x, t // 2, z, x // 2)).start()
 
-    def tick(i, carry):
-        @pl.when(i < T)
-        def _():
-            project(i)
-
-        @pl.when((y == 0) & (i < T - 2) & (i % 2 == 0))
+    def ask(t):
+        project(t)
+
+        @pl.when((y == 0) & ((t == 0) | (t == 1) | (t == 3)))
         def _():
             pl.semaphore_signal(
-                go, inc=1, device_id=at(x, i // 2 + 1, z, c), device_id_type=MESH
+                go, inc=1, device_id=at(x, (t + 3) // 2, z, c), device_id_type=MESH
             )
 
-        @pl.when(i > 1)
-        def _():
-            forward(i - 2)
-
-        @pl.when(i < T)
-        def _():
-            attend(i)
-
-        @pl.when((i > 0) & (i <= T))
-        def _():
-            back(i - 1)
-
-        return carry
-
-    lax.fori_loop(0, T + 2, tick, 0)
+    stages = (ask, attend, back, forward)
+
+    def word_of(k):
+        word = jnp.int32(0)
+        for plane, order in enumerate(ORDERS):
+            for i in range(4 * T // 8):
+                value = sum("PABF".index(s) * 4**n for n, s in enumerate(order[8 * i : 8 * i + 8]))
+                word = jnp.where((y == plane) & (k // 8 == i), value, word)
+        return word
+
+    def tick(k, state):
+        word, *counts = state
+        word = jnp.where(k % 8 == 0, word_of(k), word)
+        code = word % 4
+        for s, stage in enumerate(stages):
+            @pl.when(code == s)
+            def _():
+                stage(counts[s])
+        counts = [n + jnp.where(code == s, 1, 0) for s, n in enumerate(counts)]
+        return (word // 4, *counts)
+
+    lax.fori_loop(0, 4 * T, tick, (jnp.int32(0),) * 5)
 
     settle(raw.at[0:3], x3_s.at[0])
     settle(seg.at[0:3], x3_s.at[1])
@@ -370,12 +420,22 @@
     for k in range(3):
         settle(kvt.at[0], kv_s.at[k])
 
-    @pl.when(jnp.logical_not(self_pro))
-    def _():
-        settle(packed, pro_s.at[0])
-
-    settle(hid.at[0], pro_s.at[1])
-    settle(hid.at[0, 0:3], pro_s.at[1])
+    for h in range(2):
+        @pl.when(y == 0)
+        def _():
+            settle(h_out.at[0:7], pro_s.at[1, h])
+
+            @pl.when(jnp.logical_not(self_pro))
+            def _():
+                settle(packed.at[h], pro_s.at[0, h])
+
+        @pl.when(y > 0)
+        def _():
+            settle(h_out, pro_s.at[1, h])
+
+            @pl.when(jnp.logical_not(self_st))
+            def _():
+                settle(packed.at[h], st_s.at[h])
 
     def drain(t, carry):
         settle(q_in.at[t], q_s.at[t])
@@ -428,14 +488,15 @@
         in_specs=[any_spec, vmem, vmem, smem, vmem, any_spec, any_spec, any_spec, any_spec],
         out_specs=vmem,
         scratch_shapes=[
-            pltpu.VMEM((NX, MB, BLK), BF16),
+            pltpu.VMEM((NX, MB, 256), BF16),
             pltpu.VMEM((NX, 8, 128), I32),
             pltpu.VMEM((NX, 8, 128), I32),
             pltpu.VMEM((2, 2048, 256), BF16),
             pltpu.VMEM((4, 2, 32, 2048), BF16),
             pltpu.VMEM((2048, 256), BF16),
             pltpu.VMEM((2, 1024, BLK), BF16),
-            pltpu.VMEM((MB, BLK), BF16),
+            pltpu.VMEM((2, MB, 256), BF16),
+            pltpu.VMEM((2, MB, 256), BF16),
             pltpu.VMEM((T, 4, MB, BLK), BF16),
             pltpu.VMEM((T, 4, MB, 384), BF16),
             pltpu.VMEM((T, 3, MB, 384), BF16),
@@ -455,7 +516,7 @@
             dma((3,)),
             dma((3,)),
             dma((3,)),
-            dma((2,)),
+            dma((2, 2)),
             dma((T,)),
             dma((T,)),
             dma((T,)),
@@ -469,6 +530,8 @@
             dma((2, T)),
             dma,
             pltpu.SemaphoreType.REGULAR,
+            dma((2,)),
+            dma,
         ],
         compiler_params=pltpu.CompilerParams(
             collective_id=0, has_side_effects=True, vmem_limit_bytes=60 << 20

time: 180 us -> 174 us (0.967)
  Pallas kernels: 178 us -> 173 us
    pallas_call x1, Pallas kernels: 178 us -> 173 us  [shards(): pl.pallas_call(kernel, out_shape=jax.ShapeDtypeStruct((16, BLK), BF16), i...]
where the time goes in v3:
time: 174 us
  Pallas kernels  173 us (99%)
    pallas_call x1, Pallas kernels, shards(): pl.pallas_call(kernel, out_shape=jax.ShapeDtypeStruct((16, BLK), BF16), i...  173 us

profile of v3, /device:TPU:25, one launch (start us, length us, event | category | flops | bytes accessed | tf_op | source)
XLA Modules:
  0.0 174.2 jit_solution(18265384873415070592)
XLA Ops:
  0.0 172.9 %sections.1 = bf16[16,512]{1,0:T(8,128)(2,1)} custom-call(bf16[48,512]{1,0:T(8,128)(2,1)} %bitcast.16, s32[4,2,24]{2,1,0:T(2,128)} %row_dest.1, s32[1,4,48]{2,1,0:T(4,128)} %segs.1, s32[2,3]{1,0:T(2,128)} %bitcast.17, f32[1,8192]{1,0:T(1,128)} %gain.1, bf16[2048,256]{1,0:T(8,128)(2,1)} %bitcast.11, bf16[32,2048]{1,0:T(8,128)(2,1)} %bitcast.13, ...), custom_call_target="tpu_custom_call" | custom-call | tf_op jit(solution)/shard_map/sections/pallas_call | solution.py:485
  172.9 1.3 copy.11

commit v4 on v3

--- a/solution.py
+++ b/solution.py
@@ -107,7 +107,6 @@
     pair_z = z + 1 - 2 * odd
     self_mx = x == ring
     self_pro = (y == 0) & (x == ring) & (c == x // 2)
-    self_e = (y == 3) & (x // 2 == c)
     from_x, from_z, from_c = 2 * c + z % 2, 2 * x + z // 4, (z // 2) % 2
     self_st = (from_x == x) & (from_z == z) & (from_c == c)
     to_z = 4 * odd + 2 * c + x % 2
@@ -144,11 +143,11 @@
     def _():
         greet(at(from_x, y, from_z, from_c))
 
-    for b in range(2):
+    for xx in range(NX):
         for cc in range(2):
-            @pl.when(jnp.logical_not((y == 3) & (2 * c + b == x) & (c == cc)))
-            def _():
-                greet(at(2 * c + b, 3, z, cc))
+            @pl.when(jnp.logical_not((y == 3) & (xx == x) & (c == cc)))
+            def _():
+                greet(at(xx, 3, z, cc))
 
     seg[x] = jnp.zeros((8, 128), I32)
     seg[x, 0:4, 0:MB] = segs[0]
@@ -164,7 +163,7 @@
     code[x] = table
 
     count = 21 + jnp.where(y == 0, 3, jnp.where(self_st, 0, 1)) - self_mx.astype(I32) - self_pro.astype(I32)
-    count = count + jnp.where(y < 3, 8, 16) - self_e.astype(I32)
+    count = count + jnp.where(y < 3, 8, 31)
     pl.semaphore_wait(barrier, count)
 
     def start_pairs():
@@ -330,55 +329,61 @@
     def back(t):
         settle(mixed.at[t], mx_r.at[t])
         whole = jnp.concatenate([mixed[t, j] for j in range(8)], axis=1)
+        group = 2 * c + t % 2
+        seg_row = seg[group, pl.ds(t // 2, 1), :][:, 0:MB]
+        hits = seg_row == iota((16, MB), 0)
+        amount = jnp.maximum(jnp.sum(hits.astype(F32), axis=1, keepdims=True), 1.0)
         for jj in range(2):
             sums = dot(whole, wo_v[jj])
             kept = hid[t, 2 * odd + jj].astype(F32)
             sums = (sums + jnp.where(x == ring, kept, 0.0)).astype(BF16)
-            for i in range(2):
-                o_out[t, 2 * jj + i] = sums[:, 256 * i : 256 * i + 256]
-        for k in (2, 1, 3):
-            to = turn(k)
-            remote(
-                o_out.at[t, to], o_in.at[t, k - 1], o_s.at[t], o_r.at[t], at(to, y, z, c)
-            ).start()
+
+            @pl.when(y < 3)
+            def _():
+                for i in range(2):
+                    o_out[t, 2 * jj + i] = sums[:, 256 * i : 256 * i + 256]
+
+            @pl.when(y == 3)
+            def _():
+                e_out[t, jj] = (dot(hits.astype(BF16), sums) / amount).astype(BF16)
+                place = e_in.at[4 * x + group]
+                for k in (2, 1, 3):
+                    remote(
+                        e_out.at[t, jj], place, e_s.at[1, t], e_r, at(turn(k), t // 2, z, jj)
+                    ).start()
+                is_self = (t // 2 == 3) & (c == jj)
+
+                @pl.when(is_self)
+                def _():
+                    local(e_out.at[t, jj], place, e_r).start()
+
+                @pl.when(jnp.logical_not(is_self))
+                def _():
+                    remote(
+                        e_out.at[t, jj], place, e_s.at[0, t], e_r, at(x, t // 2, z, jj)
+                    ).start()
+
+        @pl.when(y < 3)
+        def _():
+            for k in (2, 1, 3):
+                to = turn(k)
+                remote(
+                    o_out.at[t, to], o_in.at[t, k - 1], o_s.at[t], o_r.at[t], at(to, y, z, c)
+                ).start()
 
     def forward(t):
-        settle(o_in.at[t], o_r.at[t])
-        new = o_out[t, x].astype(F32)
-        for k in range(3):
-            new = new + o_in[t, k].astype(F32)
-        new = new.astype(BF16)
-
         @pl.when(y < 3)
         def _():
-            h_out[t] = new
+            settle(o_in.at[t], o_r.at[t])
+            new = o_out[t, x].astype(F32)
+            for k in range(3):
+                new = new + o_in[t, k].astype(F32)
+            h_out[t] = new.astype(BF16)
             for dz in FAR + (0,):
                 remote(
                     h_out.at[t], hid.at[t, 2 * odd + x // 2, :, half_of(x)], h_s.at[t], h_r.at[t],
                     at(ring, y + 1, (z + dz) % NZ, c),
                 ).start()
-
-        @pl.when(y == 3)
-        def _():
-            group = 2 * c + t % 2
-            seg_row = seg[group, pl.ds(t // 2, 1), :][:, 0:MB]
-            hits = seg_row == iota((16, MB), 0)
-            amount = jnp.maximum(jnp.sum(hits.astype(F32), axis=1, keepdims=True), 1.0)
-            e_out[t] = (dot(hits.astype(BF16), new) / amount).astype(BF16)
-            place = e_in.at[x % 2, group]
-            for k in (2, 1, 3):
-                remote(
-                    e_out.at[t], place, e_s.at[1, t], e_r, at(turn(k), t // 2, z, x // 2)
-                ).start()
-            is_self = (t // 2 == 3) & (x // 2 == c)
-
-            @pl.when(is_self)
-            def _():
-                local(e_out.at[t], place, e_r).start()
-
-            @pl.when(jnp.logical_not(is_self))
-            def _():
-                remote(e_out.at[t], place, e_s.at[0, t], e_r, at(x, t // 2, z, x // 2)).start()
 
     def ask(t):
         project(t)
@@ -440,7 +445,6 @@
     def drain(t, carry):
         settle(q_in.at[t], q_s.at[t])
         settle(s_in.at[t], s_s.at[t])
-        settle(o_in.at[t], o_s.at[t])
         settle(mixed.at[t, 0:7], mx_s.at[1, t])
 
         @pl.when(jnp.logical_not(self_mx))
@@ -449,15 +453,20 @@
 
         @pl.when(y < 3)
         def _():
+            settle(o_in.at[t], o_s.at[t])
             settle(hid.at[t], h_s.at[t])
 
         @pl.when(y == 3)
         def _():
-            settle(e_in.at[0, 0:3], e_s.at[1, t])
-
-            @pl.when(jnp.logical_not((t // 2 == 3) & (x // 2 == c)))
-            def _():
-                settle(e_in.at[0, 0], e_s.at[0, t])
+            settle(e_in.at[0:6], e_s.at[1, t])
+
+            @pl.when(t // 2 < 3)
+            def _():
+                settle(e_in.at[0:2], e_s.at[0, t])
+
+            @pl.when(t // 2 == 3)
+            def _():
+                settle(e_in.at[0], e_s.at[0, t])
 
         return carry
 
@@ -466,15 +475,16 @@
     settle(e_in, e_r)
     row = iota((16, 16), 0)
     col = iota((16, 16), 1)
-    picked = [jnp.zeros((16, 256), F32) for _ in range(2)]
+    picked = jnp.zeros((16, BLK), F32)
     for g in range(NX):
         hits = ((row >> 1) & 3) == g
         hits = hits & ((row >= 8) == (col >= 3)) & (col < 6)
         hits = (hits & (code[g, 0:1, 0:16] == 2 * x + (row & 1))).astype(BF16)
-        for i in range(2):
-            picked[i] = picked[i] + dot(hits, e_in[i, g])
-    for i in range(2):
-        out[:, 256 * i : 256 * i + 256] = picked[i].astype(BF16)
+        mean = e_in[g].astype(F32)
+        for k in range(1, NX):
+            mean = mean + e_in[4 * k + g].astype(F32)
+        picked = picked + dot(hits, mean.astype(BF16))
+    out[...] = picked.astype(BF16)
 
 
 def shards(prompt_rows, row_dest, segment_ids, owner, gain, w_query, w_key, w_value, w_out):
@@ -507,8 +517,8 @@
             pltpu.VMEM((T, 4, MB, 256), BF16),
             pltpu.VMEM((T, 3, MB, 256), BF16),
             pltpu.VMEM((T, MB, 256), BF16),
-            pltpu.VMEM((T, 16, 256), BF16),
-            pltpu.VMEM((2, NX, 16, 256), BF16),
+            pltpu.VMEM((T, 2, 16, BLK), BF16),
+            pltpu.VMEM((4 * NX, 16, BLK), BF16),
             dma((5,)),
             dma((2,)),
             dma((2,)),

time: 174 us -> 172 us (0.989)
  Pallas kernels: 173 us -> 170 us
    pallas_call x1, Pallas kernels: 173 us -> 170 us  [shards(): pl.pallas_call(kernel, out_shape=jax.ShapeDtypeStruct((16, BLK), BF16), i...]
where the time goes in v4:
time: 172 us; the launch traced here: 171 us
  Pallas kernels  170 us (99%)
    pallas_call x1, Pallas kernels, shards(): pl.pallas_call(kernel, out_shape=jax.ShapeDtypeStruct((16, BLK), BF16), i...  170 us

profile of v4, /device:TPU:25, one launch (start us, length us, event | category | flops | bytes accessed | tf_op | source)
XLA Modules:
  0.0 171.3 jit_solution(7552656917155188887)
XLA Ops:
  0.0 170.0 %sections.1 = bf16[16,512]{1,0:T(8,128)(2,1)} custom-call(bf16[48,512]{1,0:T(8,128)(2,1)} %bitcast.16, s32[4,2,24]{2,1,0:T(2,128)} %row_dest.1, s32[1,4,48]{2,1,0:T(4,128)} %segs.1, s32[2,3]{1,0:T(2,128)} %bitcast.17, f32[1,8192]{1,0:T(1,128)} %gain.1, bf16[2048,256]{1,0:T(8,128)(2,1)} %bitcast.11, bf16[32,2048]{1,0:T(8,128)(2,1)} %bitcast.13, ...), custom_call_target="tpu_custom_call" | custom-call | tf_op jit(solution)/shard_map/sections/pallas_call | solution.py:495
  170.0 1.3 copy.11

commit v5 on v4

--- a/solution.py
+++ b/solution.py
@@ -270,31 +270,41 @@
     def project(t):
         settle(hid.at[t], h_r.at[t])
         squares = jnp.zeros((MB, 128), F32)
-        sums = [jnp.zeros((MB, 256), F32) for _ in range(3)]
+        gated = []
         for j in range(4):
             h = hid[t, j].astype(F32)
             square = h * h
             for i in range(4):
                 squares = squares + square[:, 128 * i : 128 * i + 128]
             g = gain[:, pl.ds(pl.multiple_of(x * 2048 + BLK * j, BLK), BLK)]
-            gated = (h * g).astype(BF16)
-            ks = slice(BLK * j, BLK * j + BLK)
-            sums[0] = sums[0] + dot(gated, wq_v[0, ks])
-            sums[1] = sums[1] + dot(gated, wq_v[1, ks])
-            sums[2] = sums[2] + dot(gated, wkv_v[ks])
+            gated.append((h * g).astype(BF16))
         total = jnp.sum(squares, axis=1, keepdims=True)
         s_out[t] = jnp.broadcast_to(to_row(total), (8, 128))
-        for r in range(NX):
-            q_out[t, r, :, 0:128] = sums[r // 2][:, 128 * (r % 2) : 128 * (r % 2) + 128].astype(BF16)
-            q_out[t, r, :, 128:384] = sums[2].astype(BF16)
         for k in (2, 1, 3):
-            to = turn(k)
             remote(
-                q_out.at[t, to], q_in.at[t, k - 1], q_s.at[t], q_r.at[t], at(to, y, z, c)
+                s_out.at[t], s_in.at[t, k - 1], s_s.at[t], s_r.at[t], at(turn(k), y, z, c)
             ).start()
-            remote(
-                s_out.at[t], s_in.at[t, k - 1], s_s.at[t], s_r.at[t], at(to, y, z, c)
-            ).start()
+
+        def times(weights):
+            sums = jnp.zeros((MB, 256), F32)
+            for j in range(4):
+                sums = sums + dot(gated[j], weights[BLK * j : BLK * j + BLK])
+            return sums.astype(BF16)
+
+        pair = times(wkv_v)
+        for jj in range(2):
+            heads = times(wq_v.at[jj])
+            for i in range(2):
+                q_out[t, 2 * jj + i, :, 0:128] = heads[:, 128 * i : 128 * i + 128]
+                q_out[t, 2 * jj + i, :, 128:384] = pair
+            for k in (2, 1, 3):
+                to = turn(k)
+
+                @pl.when(to // 2 == jj)
+                def _():
+                    remote(
+                        q_out.at[t, to], q_in.at[t, k - 1], q_s.at[t], q_r.at[t], at(to, y, z, c)
+                    ).start()
 
     def attend(t):
         settle(s_in.at[t], s_r.at[t])

time: 172 us -> 175 us (1.017)
  Pallas kernels: 170 us -> 173 us
    pallas_call x1, Pallas kernels: 170 us -> 173 us  [shards(): pl.pallas_call(kernel, out_shape=jax.ShapeDtypeStruct((16, BLK), BF16), i...]
where the time goes in v5:
time: 175 us
  Pallas kernels  173 us (99%)
    pallas_call x1, Pallas kernels, shards(): pl.pallas_call(kernel, out_shape=jax.ShapeDtypeStruct((16, BLK), BF16), i...  173 us

profile of v5, /device:TPU:25, one launch (start us, length us, event | category | flops | bytes accessed | tf_op | source)
XLA Modules:
  0.0 174.7 jit_solution(13300062691023214243)
XLA Ops:
  0.0 173.4 %sections.1 = bf16[16,512]{1,0:T(8,128)(2,1)} custom-call(bf16[48,512]{1,0:T(8,128)(2,1)} %bitcast.16, s32[4,2,24]{2,1,0:T(2,128)} %row_dest.1, s32[1,4,48]{2,1,0:T(4,128)} %segs.1, s32[2,3]{1,0:T(2,128)} %bitcast.17, f32[1,8192]{1,0:T(1,128)} %gain.1, bf16[2048,256]{1,0:T(8,128)(2,1)} %bitcast.11, bf16[32,2048]{1,0:T(8,128)(2,1)} %bitcast.13, ...), custom_call_target="tpu_custom_call" | custom-call | tf_op jit(solution)/shard_map/sections/pallas_call | solution.py:505
  173.4 1.3 copy.11
